TPU v7x, 512 devices: a whole 4x4x16 slice. The times are simulated.
512 devices in a mesh: batch: 16 (over y, x_lo, core), feat: 32 (over z, x_hi).
Axes of the slice: x: 4 (x_hi: 2, x_lo: 2; x = x_hi * 2 + x_lo), y: 4, z: 16, core: 2. Of those that a mesh axis runs over, the one named last changes fastest.
Arguments:
- first_view: bfloat16 [1024, 8192], P('batch'), may hold values from -16 to 16
- second_view: bfloat16 [1024, 8192], P('batch'), may hold values from -16 to 16
- weight: bfloat16 [8192, 8192], P('batch', 'feat'), may hold values from -0.0625 to 0.0625
Outputs:
- weight_grad: float32 [8192, 8192], P('batch', 'feat')
All inputs are finite; a program needn't handle non-finite values.
Results may differ from a plain program's by a relative error of at most 0.03.
Values may be sent and summed in bfloat16 or wider, within the bound.
A program may use at most 64 MiB of HBM per device.

v0:
```python
import jax
import jax.numpy as jnp
from jax import lax
from jax.sharding import PartitionSpec as P

off_weight = 0.0051


def normalize(values, sums, squares, count):
    mean = sums / count
    spread = squares / count - mean * mean
    scale = lax.rsqrt(spread + 1e-05)
    return (((values - mean) * scale).astype(jnp.bfloat16), scale)


def norm_backward(grad_normed, normed, scale):
    normed_wide = normed.astype(jnp.float32)
    centered = (
        grad_normed
        - jnp.mean(grad_normed, 0)
        - normed_wide * jnp.mean(grad_normed * normed_wide, 0)
    )
    return (centered * scale).astype(jnp.bfloat16)


def contract_rows(left, right):
    return lax.dot_general(
        left, right, (((0,), (0,)), ((), ())), preferred_element_type=jnp.float32
    )


def diagonal_mask(shape, row_start, col_start):
    rows_id = row_start + lax.broadcasted_iota(jnp.int32, shape, 0)
    cols_id = col_start + lax.broadcasted_iota(jnp.int32, shape, 1)
    return rows_id == cols_id


def slope_of(corr, ondiag):
    return jnp.where(ondiag, -2.0 * (1.0 - corr), 2.0 * off_weight * corr).astype(jnp.bfloat16)


def local(first_view, second_view, weight):
    rows_dev = first_view.shape[0]
    block = weight.shape[0]
    slab = weight.shape[1]
    batch_index = lax.axis_index("batch")
    feat_index = lax.axis_index("feat")
    total_rows = rows_dev * lax.axis_size("batch")
    first_block, second_block = (
        lax.all_to_all(first_view, "batch", split_axis=1, concat_axis=0, tiled=True),
        lax.all_to_all(second_view, "batch", split_axis=1, concat_axis=0, tiled=True),
    )
    piece = lax.all_gather(weight, "batch", axis=0, tiled=True)
    first_cols = first_view
    second_cols = second_view
    first_out = jnp.dot(first_cols, piece, preferred_element_type=jnp.float32)
    second_out = jnp.dot(second_cols, piece, preferred_element_type=jnp.float32)
    stats = lax.psum(
        (
            jnp.sum(first_out, 0),
            jnp.sum(first_out * first_out, 0),
            jnp.sum(second_out, 0),
            jnp.sum(second_out * second_out, 0),
        ),
        "batch",
    )
    first_normed, first_scale = normalize(first_out, stats[0], stats[1], total_rows)
    second_normed, second_scale = normalize(second_out, stats[2], stats[3], total_rows)
    first_slab, second_slab = (
        lax.all_gather(first_normed, "batch", axis=0, tiled=True),
        lax.all_gather(second_normed, "batch", axis=0, tiled=True),
    )
    first_wide, second_wide = (
        lax.all_gather(first_normed, "feat", axis=1, tiled=True),
        lax.all_gather(second_normed, "feat", axis=1, tiled=True),
    )
    first_cols, second_cols = (
        lax.all_to_all(first_wide, "batch", split_axis=1, concat_axis=0, tiled=True),
        lax.all_to_all(second_wide, "batch", split_axis=1, concat_axis=0, tiled=True),
    )
    tile_first = contract_rows(first_slab, second_cols) / total_rows
    tile_second = contract_rows(first_cols, second_slab) / total_rows
    mask_first = diagonal_mask(tile_first.shape, feat_index * slab, batch_index * block)
    mask_second = diagonal_mask(tile_second.shape, batch_index * block, feat_index * slab)
    slope_first = slope_of(tile_first, mask_first)
    slope_second = slope_of(tile_second, mask_second)
    first_part = (
        lax.dot_general(
            second_cols, slope_first, (((1,), (1,)), ((), ())), preferred_element_type=jnp.float32
        )
        / total_rows
    )
    second_part = jnp.dot(first_cols, slope_second, preferred_element_type=jnp.float32) / total_rows
    first_grad, second_grad = (
        lax.psum(first_part.astype(jnp.bfloat16), "batch").astype(jnp.float32),
        lax.psum(second_part.astype(jnp.bfloat16), "batch").astype(jnp.float32),
    )
    first_dz = norm_backward(first_grad, first_slab, first_scale)
    second_dz = norm_backward(second_grad, second_slab, second_scale)
    weight_grad = contract_rows(first_block, first_dz) + contract_rows(second_block, second_dz)
    return weight_grad * rows_dev


def solution(mesh):
    return jax.shard_map(
        local,
        mesh=mesh,
        in_specs=(P("batch", None), P("batch", None), P("batch", "feat")),
        out_specs=P("batch", "feat"),
        check_vma=False,
    )
```

profile of v0, /device:TPU:1, one launch (start us, length us, event | category | flops | bytes accessed | tf_op | source)
XLA Modules:
  0.0 584.2 jit_solution(6116969670601778659)
XLA Ops:
  6.5 0.0 copy-start.1
  6.5 0.0 all-gather.4.cloned.1.call-start
  6.5 0.7 all-gather.4.cloned.1.call-update
  7.3 0.0 all-gather.8.cloned.1.call-start
  7.3 53.0 %all-gather.4.cloned.1.call-done = bf16[8192,256]{1,0:T(8,128)(2,1)} async-done(((bf16[512,256]{1,0:T(8,128)(2,1)}), bf16[8192,256]{1,0:T(8,128)(2,1)}) %all-gather.4.cloned.1.call-update) | async-done | bytes 4194320 | tf_op jit(solution)/shard_map/all_gather | solution.py:53
  60.3 0.0 copy-start
  60.3 3.5 fusion.41
  63.8 0.0 copy-done.1
  63.8 0.3 copy-done
  64.1 0.8 fusion.42
  64.9 26.8 %all-reduce = (f32[256]{0:T(256)S(1)}, f32[256]{0:T(256)S(1)}, f32[256]{0:T(256)S(1)}, f32[256]{0:T(256)S(1)}) all-reduce(f32[256]{0:T(256)S(1)} %get-tuple-element.12, f32[256]{0:T(256)S(1)} %get-tuple-element.11, f32[256]{0:T(256)S(1)} %get-tuple-element.10, ...), channel_id=1, replica_groups=mesh['batch'=16,'feat'=32] {'batch'}, use_global_device_ids=true, to_apply=%region_7.0 | all-reduce | flops 1024 | bytes 8192 | tf_op jit(solution)/shard_map/psum | solution.py:58
  91.7 0.6 multiply_convert_fusion
  92.3 0.0 all-gather.8.cloned.1.call-update
  92.3 0.0 all-gather.6.cloned.1.call-start
  92.4 0.6 multiply_convert_fusion.1
  93.0 0.1 all-gather.6.cloned.1.call-update
  93.1 125.7 %all-gather.8.cloned.1.call-done = bf16[64,8192]{1,0:T(8,128)(2,1)} async-done(((bf16[64,256]{1,0:T(8,128)(2,1)}), bf16[64,8192]{1,0:T(8,128)(2,1)}) %all-gather.8.cloned.1.call-update) | async-done | bytes 1048592 | tf_op jit(solution)/shard_map/all_gather | solution.py:74
  218.8 0.0 copy-start.4
  218.8 0.0 copy-start.3
  218.8 2.3 copy.27
  221.1 15.1 %all-to-all-start.2 = ((bf16[64,16,512]{2,0,1:T(8,128)(2,1)}), bf16[64,16,512]{2,0,1:T(8,128)(2,1)S(1)}, u32[]{:S(2)}, u32[]{:S(2)}) async-start(bf16[64,16,512]{2,0,1:T(8,128)(2,1)} %bitcast.39), calls=%async_computation.2 | async-start | bytes 2097152 | tf_op jit(solution)/shard_map/all_to_all | solution.py:78
  236.2 115.3 %all-gather.6.cloned.1.call-done = bf16[64,8192]{1,0:T(8,128)(2,1)} async-done(((bf16[64,256]{1,0:T(8,128)(2,1)}), bf16[64,8192]{1,0:T(8,128)(2,1)}) %all-gather.6.cloned.1.call-update) | async-done | bytes 1048592 | tf_op jit(solution)/shard_map/all_gather | solution.py:75
  351.5 2.3 copy.29
  353.8 0.0 all-to-all-done.2
  353.8 15.1 %all-to-all-start = ((bf16[64,16,512]{2,0,1:T(8,128)(2,1)}), bf16[64,16,512]{2,0,1:T(8,128)(2,1)}, u32[]{:S(2)}, u32[]{:S(2)}) async-start(bf16[64,16,512]{2,0,1:T(8,128)(2,1)} %bitcast.41), calls=%async_computation | async-start | bytes 2097152 | tf_op jit(solution)/shard_map/all_to_all | solution.py:79
  368.9 0.0 all-reduce.4.cloned.1.call-start
  369.0 0.0 copy-done.4
  369.0 29.5 %all_gather.19 = bf16[1024,256]{1,0:T(8,128)(2,1)S(1)} all-gather(bf16[64,256]{1,0:T(8,128)(2,1)S(1)} %copy-done.4), channel_id=1, replica_groups=mesh['batch'=16,'feat'=32] {'batch'}, dimensions={0}, use_global_device_ids=true | all-gather | bytes 557056 | tf_op jit(solution)/shard_map/all_gather | solution.py:71
  398.5 0.0 copy-done.3
  398.5 19.7 %all_gather.17 = bf16[1024,256]{1,0:T(8,128)(2,1)S(1)} all-gather(bf16[64,256]{1,0:T(8,128)(2,1)S(1)} %copy-done.3), channel_id=1, replica_groups=mesh['batch'=16,'feat'=32] {'batch'}, dimensions={0}, use_global_device_ids=true | all-gather | bytes 557056 | tf_op jit(solution)/shard_map/all_gather | solution.py:70
  418.2 2.1 fusion.1
  420.3 0.0 all-to-all-done
  420.3 0.0 copy-start.2
  420.3 3.4 fusion
  423.7 0.0 all-reduce.4.cloned.1.call-update
  423.7 1.1 copy.28
  424.9 3.6 all-to-all-start.1
  428.4 0.0 copy-done.2
  428.5 1.1 copy.26
  429.5 122.2 %all-reduce.4.cloned.1.call-done = (bf16[1024,256]{1,0:T(8,128)(2,1)}, bf16[1024,256]{1,0:T(8,128)(2,1)}) async-done(((bf16[1024,256]{1,0:T(8,128)(2,1)}, bf16[1024,256]{1,0:T(8,128)(2,1)}), (bf16[1024,256]{1,0:T(8,128)(2,1)}, bf16[1024,256]{1,0:T(8,128)(2,1)})) %all-reduce.4.cloned.1.call-update) | async-done | bytes 1048592 | tf_op jit(solution)/shard_map/psum | solution.py:95
  551.8 1.6 convert_reduce_fusion
  553.3 0.0 all-to-all-done.1
  553.4 5.8 all-to-all-start.3
  559.2 2.3 fusion.13
  561.5 13.4 %all-to-all-done.3 = bf16[64,16,512]{2,0,1:T(8,128)(2,1)S(1)} async-done(((bf16[64,16,512]{2,0,1:T(8,128)(2,1)}), bf16[64,16,512]{2,0,1:T(8,128)(2,1)S(1)}, u32[]{:S(2)}, u32[]{:S(2)}) %all-to-all-start.3) | async-done | bytes 1048608 | tf_op jit(solution)/shard_map/all_to_all | solution.py:51
  575.0 1.7 fusion.3
  576.7 1.0 copy.17
  (8 shorter events, 0.0 us)
Async XLA Ops:
  6.5 57.3 %copy-start.1 = (bf16[64,8192]{1,0:T(8,128)(2,1)S(1)}, bf16[64,8192]{1,0:T(8,128)(2,1)}, u32[]{:S(2)}) copy-start(bf16[64,8192]{1,0:T(8,128)(2,1)} %param.3) | copy-start | bytes 3145732
  6.5 53.8 %all-gather.4.cloned.1.call-start = ((), (), s32[]{:S(2)}) async-start(), calls=%async_computation.4 | async-start | bytes 4456448 | tf_op jit(solution)/shard_map/all_gather | solution.py:53
  7.3 211.5 %all-gather.8.cloned.1.call-start = ((), (), s32[]{:S(2)}) async-start(), calls=%async_computation.6 | async-start | bytes 1081344 | tf_op jit(solution)/shard_map/all_gather | solution.py:74
  60.3 3.7 copy-start
  92.3 259.2 %all-gather.6.cloned.1.call-start = ((), (), s32[]{:S(2)}) async-start(), calls=%async_computation.5 | async-start | bytes 1081344 | tf_op jit(solution)/shard_map/all_gather | solution.py:75
  218.8 150.2 %copy-start.4 = (bf16[64,256]{1,0:T(8,128)(2,1)S(1)}, bf16[64,256]{1,0:T(8,128)(2,1)}, u32[]{:S(2)}) copy-start(bf16[64,256]{1,0:T(8,128)(2,1)} %multiply_convert_fusion.1) | copy-start | bytes 98308
  218.8 179.8 %copy-start.3 = (bf16[64,256]{1,0:T(8,128)(2,1)S(1)}, bf16[64,256]{1,0:T(8,128)(2,1)}, u32[]{:S(2)}) copy-start(bf16[64,256]{1,0:T(8,128)(2,1)} %multiply_convert_fusion) | copy-start | bytes 98308
  221.1 132.7 %all-to-all-start.2 = ((bf16[64,16,512]{2,0,1:T(8,128)(2,1)}), bf16[64,16,512]{2,0,1:T(8,128)(2,1)S(1)}, u32[]{:S(2)}, u32[]{:S(2)}) async-start(bf16[64,16,512]{2,0,1:T(8,128)(2,1)} %bitcast.39), calls=%async_computation.2 | async-start | bytes 2097152 | tf_op jit(solution)/shard_map/all_to_all | solution.py:78
  353.8 66.5 %all-to-all-start = ((bf16[64,16,512]{2,0,1:T(8,128)(2,1)}), bf16[64,16,512]{2,0,1:T(8,128)(2,1)}, u32[]{:S(2)}, u32[]{:S(2)}) async-start(bf16[64,16,512]{2,0,1:T(8,128)(2,1)} %bitcast.41), calls=%async_computation | async-start | bytes 2097152 | tf_op jit(solution)/shard_map/all_to_all | solution.py:79
  368.9 182.9 %all-reduce.4.cloned.1.call-start = ((), (), s32[]{:S(2)}) async-start(), calls=%async_computation.7 | async-start | bytes 2097152 | tf_op jit(solution)/shard_map/psum | solution.py:95
  420.3 8.1 %copy-start.2 = (bf16[64,8192]{1,0:T(8,128)(2,1)S(1)}, bf16[64,8192]{1,0:T(8,128)(2,1)}, u32[]{:S(2)}) copy-start(bf16[64,8192]{1,0:T(8,128)(2,1)} %param.4) | copy-start | bytes 3145732
  424.9 128.5 %all-to-all-start.1 = ((bf16[64,16,512]{2,0,1:T(8,128)(2,1)}), bf16[64,16,512]{2,0,1:T(8,128)(2,1)S(1)}, u32[]{:S(2)}, u32[]{:S(2)}) async-start(bf16[64,16,512]{2,0,1:T(8,128)(2,1)} %bitcast.40), calls=%async_computation.1 | async-start | bytes 2097152 | tf_op jit(solution)/shard_map/all_to_all | solution.py:50
  553.4 21.6 %all-to-all-start.3 = ((bf16[64,16,512]{2,0,1:T(8,128)(2,1)}), bf16[64,16,512]{2,0,1:T(8,128)(2,1)S(1)}, u32[]{:S(2)}, u32[]{:S(2)}) async-start(bf16[64,16,512]{2,0,1:T(8,128)(2,1)} %bitcast.38), calls=%async_computation.3 | async-start | bytes 2097152 | tf_op jit(solution)/shard_map/all_to_all | solution.py:51
Sparse Core Ops, SparseCore 0:
  9.5 50.7 all-gather.3
  92.5 126.2 all-gather.7
  221.7 129.8 all-gather.5
  423.9 127.8 all-reduce.3
where the time goes:
time: 585 us; the launch traced here: 584 us
  waiting for transfers between devices  431 us (74%)
  blocking collectives  76 us (13%)
  starting transfers between devices  39.7 us (7%)
  matrix products  13.8 us (2%)
  between operations  13.2 us (2%)
  local copies, waits for them, and re-layouts  8.12 us (1%)
    all_gather x1, waiting for transfers between devices, local(): lax.all_gather(first_normed, 'feat', axis=1, tiled=True)  126 us
    psum x1, waiting for transfers between devices, local(): lax.psum(first_part.astype(jnp.bfloat16), 'batch').astype(jnp.float32)  122 us
    all_gather x1, waiting for transfers between devices, local(): lax.all_gather(second_normed, 'feat', axis=1, tiled=True)  115 us
    all_gather x1, waiting for transfers between devices, local(): piece = lax.all_gather(weight, 'batch', axis=0, tiled=True)  53 us
    all_gather x1, blocking collectives, local(): lax.all_gather(second_normed, 'batch', axis=0, tiled=True)  29.5 us
    psum x1, blocking collectives, local(): lax.psum((jnp.sum(first_out, 0), jnp.sum(first_out * first_out, 0), jnp.s...  26.8 us
    all_gather x1, blocking collectives, local(): lax.all_gather(first_normed, 'batch', axis=0, tiled=True)  19.7 us
    all_to_all x1, starting transfers between devices, local(): lax.all_to_all(second_wide, 'batch', split_axis=1, concat_axis=0, tiled=T...  15.1 us
  transfers between devices with their start and end apart: 8, of which 5 were waited for; matrix products, arithmetic and copies ran while one was open for 2% of the time, Pallas kernels for 0%

commit v1 on v0

v1 whole, which is shorter than its diff:
```python
import functools

import jax
import jax.numpy as jnp
from jax import lax
from jax.experimental import pallas as pl
from jax.experimental.pallas import tpu as pltpu
from jax.sharding import PartitionSpec as P

MESH = pl.DeviceIdType.MESH
off_weight = 0.0051
NX, NY, NZ = 4, 4, 16
ROWS = 1024
BLOCK = 512
SLAB = 256
PAIR = 2 * BLOCK
PAIRS = 8
OWN = SLAB // PAIRS
STRIP = ROWS // (NX * NY)
BF = jnp.bfloat16
F32 = jnp.float32

ROW_DIMS = (((1,), (1,)), ((), ()))


def coords():
    b = lax.axis_index("batch")
    f = lax.axis_index("feat")
    return (f % 2) * 2 + (b // 2) % 2, b // 4, f // 2, b % 2


def dev(x, y, z, core):
    return ((y * 2 + x % 2) * 2 + core, z * 2 + x // 2)


def rcopy(src, dst, send, recv, device):
    return pltpu.make_async_remote_copy(
        src_ref=src, dst_ref=dst, send_sem=send, recv_sem=recv, device_id=device, device_id_type=MESH
    )


def kernel(
    first, second, w, out,
    xb, xt, wb, wt, pt, ptb, rsb, nt, sc, scb, noth, kl, kp, zb, ks, kf, gs, gb, nn, no, gw, cb, fs, fr,
    loc, x_s, x_r, w_s, w_r, rs_s, rs_r, ag_s, ag_r, sc_s, sc_r, n_s, n_r, zr_s, zr_r, za_s, za_r, g_s, g_r, f_s, f_r,
):
    x, y, z, core = coords()
    xlo, xhi = x % 2, x // 2
    pair = y * 2 + xlo
    place = y * NX + x
    sib = dev(x, y, z, 1 - core)

    barrier = pltpu.get_barrier_semaphore()
    pl.semaphore_signal(barrier, 1, device_id=sib, device_id_type=MESH)

    @pl.loop(1, NX * NY)
    def _(i):
        for c in range(2):
            pl.semaphore_signal(
                barrier, 1, device_id=dev((x + i % NX) % NX, (y + i // NX) % NY, z, c), device_id_type=MESH
            )

    @pl.loop(1, NZ)
    def _(i):
        for c in range(2):
            pl.semaphore_signal(barrier, 1, device_id=dev(x, y, (z + i) % NZ, c), device_id_type=MESH)

    pl.semaphore_wait(barrier, 1 + 2 * (NX * NY - 1) + 2 * (NZ - 1))

    mine = pair * 2 + core

    def x_copy(view, dy, dlo, target):
        ty = (y + dy) % NY
        tlo = (xlo + dlo) % 2
        tx = x if dlo == 0 else (x ^ 1 if view == 0 else 3 - x)
        src = (first, second)[view]
        col = pl.multiple_of((ty * 2 + tlo) * PAIR, PAIR)
        return rcopy(
            src.at[:, pl.ds(col, PAIR)],
            xb.at[pl.ds(pl.multiple_of(mine * 64, 64), 64), :],
            x_s.at[(dy * 2 + dlo) * 2 + view],
            x_r.at[mine],
            dev(tx, ty, z, view) if target is None else target,
        )

    def own_copy(view):
        src = (first, second)[view]
        return pltpu.make_async_copy(
            src.at[:, pl.ds(pl.multiple_of(pair * PAIR, PAIR), PAIR)],
            xb.at[pl.ds(pl.multiple_of(mine * 64, 64), 64), :],
            loc.at[0],
        )

    offsets = [(dy, dlo) for dy in (2, 1, 3, 0) for dlo in (1, 0) if (dy, dlo) != (0, 0)]
    for dy, dlo in offsets:
        for view in range(2):
            x_copy(view, dy, dlo, None).start()
    for view in range(2):
        @pl.when(core == view)
        def _():
            own_copy(view).start()

        @pl.when(core != view)
        def _():
            x_copy(view, 0, 0, sib).start()

    w_place = wb.at[pl.ds(pl.multiple_of(core * BLOCK, BLOCK), BLOCK), :]
    w_copy = rcopy(w, w_place, w_s, w_r, sib)
    w_copy.start()
    w_own = pltpu.make_async_copy(w, w_place, loc.at[1])
    w_own.start()
    w_own.wait()
    w_copy.wait()
    for i in range(PAIR // SLAB):
        wt[:, i * SLAB:(i + 1) * SLAB] = wb[i * SLAB:(i + 1) * SLAB, :].T
    for view in range(2):
        @pl.when(core == view)
        def _():
            own_copy(view).wait()

    def chunk_step(dy, dlo):
        chunk = ((y + dy) % NY) * 2 + (xlo + dlo) % 2
        for c in range(2):
            b = chunk * 2 + c
            rows = pl.ds(pl.multiple_of(b * 64, 64), 64)

            @pl.when(b != mine)
            def _():
                rcopy(xb.at[rows, :], xb.at[rows, :], x_s.at[0], x_r.at[b], sib).wait_recv()

        rows = pl.ds(pl.multiple_of(chunk * 128, 128), 128)
        xs = xb[rows, :]
        pt[:, rows] = lax.dot_general(wt[...], xs, ROW_DIMS, preferred_element_type=F32)
        xt[:, rows] = xs.T

    for dy, dlo in [(0, 0), (0, 1), (1, 0), (3, 0), (1, 1), (3, 1), (2, 0), (2, 1)]:
        chunk_step(dy, dlo)

    for i in range(PAIRS):
        part = pt[i * OWN:(i + 1) * OWN, :]
        ptb[i * OWN:(i + 1) * OWN, :] = (part - jnp.mean(part, 1, keepdims=True)).astype(BF)

    def rs_copy(i):
        ty = (y + i // 2) % NY
        tlo = (xlo + i % 2) % 2
        rows = pl.ds(pl.multiple_of((ty * 2 + tlo) * OWN, OWN), OWN)
        return rcopy(
            ptb.at[rows, :], rsb.at[pair], rs_s.at[i], rs_r.at[pair], dev(xhi * 2 + tlo, ty, z, core)
        )

    @pl.loop(1, PAIRS)
    def _(i):
        rs_copy(i).start()

    rsb[pair] = ptb[pl.ds(pl.multiple_of(pair * OWN, OWN), OWN), :]

    @pl.loop(1, PAIRS)
    def _(i):
        other = (pair + i) % PAIRS
        rcopy(rsb.at[other], rsb.at[other], rs_s.at[0], rs_r.at[other], sib).wait_recv()

    total = rsb[0].astype(F32)
    for i in range(1, PAIRS):
        total = total + rsb[i].astype(F32)
    mean = jnp.sum(total, 1, keepdims=True) / ROWS
    spread = jnp.sum(total * total, 1, keepdims=True) / ROWS - mean * mean
    scale = lax.rsqrt(spread + 1e-05)
    own_rows = pl.ds(pl.multiple_of(xhi * SLAB + pair * OWN, OWN), OWN)
    nt[own_rows, :] = ((total - mean) * scale).astype(BF)
    lane = lax.broadcasted_iota(jnp.int32, (8, 128), 1)
    wide = jnp.broadcast_to(scale, (OWN, 128))
    tile = wide[0:8]
    for i in range(1, OWN // 8):
        tile = jnp.where(lane >= 32 * i, wide[8 * i:8 * i + 8], tile)
    sc[pair] = tile

    def ag_copy(i):
        return rcopy(
            nt.at[own_rows, :], nt.at[own_rows, :], ag_s.at[i], ag_r.at[place],
            dev((x + i % NX) % NX, (y + i // NX) % NY, z, core),
        )

    def sc_copy(i):
        return rcopy(
            sc.at[pair], sc.at[pair], sc_s.at[i], sc_r.at[pair],
            dev(xhi * 2 + (xlo + i % 2) % 2, (y + i // 2) % NY, z, core),
        )

    @pl.loop(1, NX * NY)
    def _(i):
        ag_copy(i).start()

    @pl.loop(1, PAIRS)
    def _(i):
        sc_copy(i).start()

    @pl.loop(1, NX * NY)
    def _(i):
        sx, sy = (x + i % NX) % NX, (y + i // NX) % NY
        rows = pl.ds(pl.multiple_of((sx // 2) * SLAB + (sy * 2 + sx % 2) * OWN, OWN), OWN)
        rcopy(nt.at[rows, :], nt.at[rows, :], ag_s.at[0], ag_r.at[sy * NX + sx], sib).wait_recv()

    kl[...] = nt[:, pl.ds(pl.multiple_of((place // 2) * 128, 128), 128)].T
    strip = kl[pl.ds(pl.multiple_of((place % 2) * STRIP, STRIP), STRIP), :]
    for i in range(4):
        kp[:, i * 256:(i + 1) * 256] = jnp.dot(
            strip, nt[:, i * 256:(i + 1) * 256], preferred_element_type=F32
        ).astype(BF)

    def piece(ref, t):
        return ref.at[pl.ds(pl.multiple_of((t // 4) * 16, 16), 16), pl.ds(pl.multiple_of((t % 4) * 256, 256), 256)]

    def zr_copy(i):
        t = (z + i) % NZ
        return rcopy(piece(kp, t), zb.at[z], zr_s.at[i], zr_r.at[z], dev(x, y, t, core))

    @pl.loop(1, NZ)
    def _(i):
        zr_copy(i).start()

    slab_rows = pl.ds(pl.multiple_of(xhi * SLAB, SLAB), SLAB)
    n_copy = rcopy(nt.at[slab_rows, :], noth, n_s, n_r, sib)
    n_copy.start()

    zb[z] = kp[
        pl.ds(pl.multiple_of((z // 4) * 16, 16), 16), pl.ds(pl.multiple_of((z % 4) * 256, 256), 256)
    ]

    @pl.loop(1, NZ)
    def _(i):
        t = (z + i) % NZ
        rcopy(zb.at[t], zb.at[t], zr_s.at[0], zr_r.at[t], sib).wait_recv()

    acc = zb[0].astype(F32)
    for i in range(1, NZ):
        acc = acc + zb[i].astype(F32)
    ks[...] = acc.astype(BF)

    def za_copy(i):
        return rcopy(ks, piece(kf, z), za_s.at[i], za_r.at[z], dev(x, y, (z + i) % NZ, 1 - core))

    @pl.loop(0, NZ)
    def _(i):
        za_copy(i).start()

    n_copy.wait()
    for i in range(8):
        rows = slice(i * 128, (i + 1) * 128)
        nn[rows, :] = nt[slab_rows, rows].T
        no[rows, :] = noth[:, rows].T
    diag = jnp.zeros((1, SLAB), F32)
    for i in range(8):
        rows = slice(i * 128, (i + 1) * 128)
        diag = diag + jnp.sum(nn[rows, :].astype(F32) * no[rows, :].astype(F32), 0, keepdims=True)
    diag = diag / ROWS
    d = -2.0 * (1.0 - diag) - 2.0 * off_weight * diag

    @pl.loop(1, PAIRS)
    def _(i):
        other = (pair + i) % PAIRS
        rcopy(sc.at[other], sc.at[other], sc_s.at[0], sc_r.at[other], sib).wait_recv()

    cols = []
    for i in range(PAIRS):
        t = sc[i]
        for j in range(OWN // 8):
            cols.append(jnp.broadcast_to(t[:, 32 * j:32 * j + 1], (8, 128)))
    scale_row = jnp.concatenate(cols, 0).T[0:1, :]

    @pl.loop(0, NZ)
    def _(i):
        t = (z + i) % NZ
        rcopy(ks, piece(kf, t), za_s.at[0], za_r.at[t], sib).wait_recv()

    for h in range(2):
        gs[h] = lax.dot_general(
            kf[...], nt[h * SLAB:(h + 1) * SLAB, :], ROW_DIMS, preferred_element_type=F32
        ).astype(BF)

    def g_copy(i):
        tx = (x + i % NX) % NX
        return rcopy(
            gs.at[tx // 2], gb.at[pl.ds(pl.multiple_of(place * STRIP, STRIP), STRIP), :], g_s.at[i], g_r.at[place],
            dev(tx, (y + i // NX) % NY, z, core),
        )

    @pl.loop(1, NX * NY)
    def _(i):
        g_copy(i).start()

    gb[pl.ds(pl.multiple_of(place * STRIP, STRIP), STRIP), :] = gs[xhi]

    @pl.loop(1, NX * NY)
    def _(i):
        t = ((y + i // NX) % NY) * NX + (x + i % NX) % NX
        rows = pl.ds(pl.multiple_of(t * STRIP, STRIP), STRIP)
        rcopy(gb.at[rows, :], gb.at[rows, :], g_s.at[0], g_r.at[t], sib).wait_recv()

    g_sum = jnp.zeros((1, SLAB), F32)
    gn_sum = jnp.zeros((1, SLAB), F32)
    for i in range(8):
        rows = slice(i * 128, (i + 1) * 128)
        g = gb[rows, :].astype(F32) * (2.0 * off_weight / ROWS) + no[rows, :].astype(F32) * d
        gw[rows, :] = g
        g_sum = g_sum + jnp.sum(g, 0, keepdims=True)
        gn_sum = gn_sum + jnp.sum(g * nn[rows, :].astype(F32), 0, keepdims=True)
    g_mean = g_sum / ROWS
    gn_mean = gn_sum / ROWS
    for i in range(8):
        rows = slice(i * 128, (i + 1) * 128)
        cb[rows, :] = (gw[rows, :] - g_mean - nn[rows, :].astype(F32) * gn_mean).astype(BF)

    factor = scale_row * (64.0 / ROWS)

    def product(block, i):
        rows = pl.ds(pl.multiple_of(block * BLOCK + i * 128, 128), 128)
        return jnp.dot(xt[rows, :], cb[...], preferred_element_type=F32) * factor

    for i in range(4):
        fs[i * 128:(i + 1) * 128, :] = product(1 - core, i)
    f_copy = rcopy(fs, fr, f_s, f_r, sib)
    f_copy.start()
    for i in range(4):
        out[i * 128:(i + 1) * 128, :] = product(core, i)
    f_copy.wait()
    out[...] += fr[...]

    for dy, dlo in offsets:
        for view in range(2):
            x_copy(view, dy, dlo, None).wait_send()
    for view in range(2):
        @pl.when(core != view)
        def _():
            x_copy(view, 0, 0, sib).wait_send()

    @pl.loop(1, PAIRS)
    def _(i):
        rs_copy(i).wait_send()
        sc_copy(i).wait_send()

    @pl.loop(1, NX * NY)
    def _(i):
        ag_copy(i).wait_send()
        g_copy(i).wait_send()

    @pl.loop(1, NZ)
    def _(i):
        zr_copy(i).wait_send()

    @pl.loop(0, NZ)
    def _(i):
        za_copy(i).wait_send()


def local(first_view, second_view, weight):
    dma = pltpu.SemaphoreType.DMA
    vm = pltpu.VMEM
    return pl.pallas_call(
        kernel,
        out_shape=jax.ShapeDtypeStruct((BLOCK, SLAB), F32),
        in_specs=[pl.BlockSpec(memory_space=pl.ANY)] * 3,
        out_specs=pl.BlockSpec(memory_space=pltpu.VMEM),
        scratch_shapes=[
            vm((ROWS, PAIR), BF), vm((PAIR, ROWS), BF), vm((PAIR, SLAB), BF), vm((SLAB, PAIR), BF),
            vm((SLAB, ROWS), F32), vm((SLAB, ROWS), BF), vm((PAIRS, OWN, ROWS), BF), vm((2 * SLAB, ROWS), BF),
            vm((PAIRS, 8, 128), F32), vm((8, 128), F32), vm((SLAB, ROWS), BF), vm((128, 2 * SLAB), BF),
            vm((STRIP, ROWS), BF), vm((NZ, 16, 256), BF), vm((16, 256), BF), vm((STRIP, ROWS), BF),
            vm((2, STRIP, SLAB), BF), vm((ROWS, SLAB), BF), vm((ROWS, SLAB), BF), vm((ROWS, SLAB), BF),
            vm((ROWS, SLAB), F32), vm((ROWS, SLAB), BF), vm((BLOCK, SLAB), F32), vm((BLOCK, SLAB), F32),
            dma((2,)), dma((16,)), dma((16,)), dma, dma, dma((PAIRS,)), dma((PAIRS,)), dma((16,)), dma((16,)),
            dma((PAIRS,)), dma((PAIRS,)), dma, dma, dma((NZ,)), dma((NZ,)), dma((NZ,)), dma((NZ,)),
            dma((16,)), dma((16,)), dma, dma,
        ],
        compiler_params=pltpu.CompilerParams(collective_id=0, has_side_effects=True, vmem_limit_bytes=48 << 20),
        cost_estimate=pl.CostEstimate(flops=4 * 10**9, bytes_accessed=4 << 20, transcendentals=0),
    )(first_view, second_view, weight)


def solution(mesh):
    return jax.shard_map(
        local,
        mesh=mesh,
        in_specs=(P("batch", None), P("batch", None), P("batch", "feat")),
        out_specs=P("batch", "feat"),
        check_vma=False,
    )
```

time: 585 us -> 109 us (0.19)
  waiting for transfers between devices: 431 us -> 0 us
  Pallas kernels: 0 us -> 105 us
  blocking collectives: 76 us -> 0 us
  starting transfers between devices: 39.7 us -> 0 us
  matrix products: 13.8 us -> 0 us
  between operations: 13.2 us -> 0.01 us
    all_gather x3 -> x0, waiting for transfers between devices: 294 us -> none  [the longest x1 126 us: local(): lax.all_gather(first_normed, 'feat', axis=1, tiled=True)]
    psum x1 -> x0, waiting for transfers between devices: 122 us -> none  [local(): lax.psum(first_part.astype(jnp.bfloat16), 'batch').astype(jnp.float32)]
    pallas_call x0 -> x1, Pallas kernels: none -> 105 us  [local(): pl.pallas_call(kernel, out_shape=jax.ShapeDtypeStruct((BLOCK, SLAB), F32)...]
    all_gather x2 -> x0, blocking collectives: 49.2 us -> none  [the longest x1 29.5 us: local(): lax.all_gather(second_normed, 'batch', axis=0, tiled=True)]
    all_to_all x4 -> x0, starting transfers between devices: 39.5 us -> none  [the longest x1 15.1 us: local(): lax.all_to_all(second_wide, 'batch', split_axis=1, concat_axis=0, tiled=T...]
    psum x1 -> x0, blocking collectives: 26.8 us -> none  [local(): lax.psum((jnp.sum(first_out, 0), jnp.sum(first_out * first_out, 0), jnp.s...]
    dot_general x6 -> x0, matrix products: 13.8 us -> none  [the longest x2 4.05 us: contract_rows(): lax.dot_general(left, right, (((0,), (0,)), ((), ())), preferred_element_...]
    all_to_all x4 -> x0, waiting for transfers between devices: 13.5 us -> none  [the longest x1 13.4 us: local(): lax.all_to_all(second_view, 'batch', split_axis=1, concat_axis=0, tiled=T...]
  transfers between devices with their start and end apart: 8 -> 0, of which waited for: 5 -> 0; matrix products, arithmetic and copies ran while one was open for 2% -> 0% of each run, Pallas kernels for 0% -> 0%
where the time goes in v1:
time: 109 us
  Pallas kernels  105 us (96%)
  local copies, waits for them, and re-layouts  4.19 us (4%)
    pallas_call x1, Pallas kernels, local(): pl.pallas_call(kernel, out_shape=jax.ShapeDtypeStruct((BLOCK, SLAB), F32)...  105 us
    unnamed x7, local copies, waits for them, and re-layouts  4.19 us

profile of v1, /device:TPU:1, one launch (start us, length us, event | category | flops | bytes accessed | tf_op | source)
XLA Modules:
  0.0 109.0 jit_solution(7422436122494375785)
XLA Ops:
  0.0 0.0 copy-start
  0.0 1.2 %copy-done = bf16[64,8192]{1,0:T(8,128)(2,1)S(1)} copy-done((bf16[64,8192]{1,0:T(8,128)(2,1)S(1)}, bf16[64,8192]{1,0:T(8,128)(2,1)}, u32[]{:S(2)}) %copy-start) | copy-done | bytes 1048600
  1.2 0.0 copy-start.1
  1.2 1.2 %copy-done.1 = bf16[64,8192]{1,0:T(8,128)(2,1)S(1)} copy-done((bf16[64,8192]{1,0:T(8,128)(2,1)S(1)}, bf16[64,8192]{1,0:T(8,128)(2,1)}, u32[]{:S(2)}) %copy-start.1) | copy-done | bytes 1048600
  2.5 0.0 copy-start.2
  2.5 0.9 copy-done.2
  3.4 104.8 %shard_map.37 = f32[512,256]{1,0:T(8,128)S(1)} custom-call(bf16[64,8192]{1,0:T(8,128)(2,1)S(1)} %copy-done, bf16[64,8192]{1,0:T(8,128)(2,1)S(1)} %copy-done.1, bf16[512,256]{1,0:T(8,128)(2,1)S(1)} %copy-done.2), custom_call_target="tpu_custom_call" | custom-call | flops 4000000000 | bytes 4194304 | tf_op jit(solution)/shard_map/pallas_call | solution.py:358
  108.2 0.8 copy.5
Async XLA Ops:
  0.0 1.2 %copy-start = (bf16[64,8192]{1,0:T(8,128)(2,1)S(1)}, bf16[64,8192]{1,0:T(8,128)(2,1)}, u32[]{:S(2)}) copy-start(bf16[64,8192]{1,0:T(8,128)(2,1)} %first.1) | copy-start | bytes 3145732
  1.2 1.2 %copy-start.1 = (bf16[64,8192]{1,0:T(8,128)(2,1)S(1)}, bf16[64,8192]{1,0:T(8,128)(2,1)}, u32[]{:S(2)}) copy-start(bf16[64,8192]{1,0:T(8,128)(2,1)} %second.1) | copy-start | bytes 3145732
  2.5 0.9 copy-start.2

commit v2 on v1

--- a/solution.py
+++ b/solution.py
@@ -26,11 +26,19 @@
 def coords():
     b = lax.axis_index("batch")
     f = lax.axis_index("feat")
-    return (f % 2) * 2 + (b // 2) % 2, b // 4, f // 2, b % 2
+    return (f & 1) * 2 + ((b >> 1) & 1), b >> 2, f >> 1, b & 1
 
 
 def dev(x, y, z, core):
-    return ((y * 2 + x % 2) * 2 + core, z * 2 + x // 2)
+    return (y * 4 + (x & 1) * 2 + core, z * 2 + (x >> 1))
+
+
+def each(low, high):
+    def run(body):
+        for i in range(low, high):
+            body(i)
+
+    return run
 
 
 def rcopy(src, dst, send, recv, device):
@@ -45,33 +53,42 @@
     loc, x_s, x_r, w_s, w_r, rs_s, rs_r, ag_s, ag_r, sc_s, sc_r, n_s, n_r, zr_s, zr_r, za_s, za_r, g_s, g_r, f_s, f_r,
 ):
     x, y, z, core = coords()
-    xlo, xhi = x % 2, x // 2
+    xlo, xhi = x & 1, x >> 1
     pair = y * 2 + xlo
     place = y * NX + x
     sib = dev(x, y, z, 1 - core)
+    sent = []
+
+    def when_sent(copy, low, high):
+        def wait():
+            @each(low, high)
+            def _(i):
+                copy(i).wait_send()
+
+        sent.append(wait)
 
     barrier = pltpu.get_barrier_semaphore()
     pl.semaphore_signal(barrier, 1, device_id=sib, device_id_type=MESH)
 
-    @pl.loop(1, NX * NY)
+    @each(1, NX * NY)
     def _(i):
         for c in range(2):
             pl.semaphore_signal(
-                barrier, 1, device_id=dev((x + i % NX) % NX, (y + i // NX) % NY, z, c), device_id_type=MESH
+                barrier, 1, device_id=dev((x + i) & 3, (y + (i >> 2)) & 3, z, c), device_id_type=MESH
             )
 
-    @pl.loop(1, NZ)
+    @each(1, NZ)
     def _(i):
         for c in range(2):
-            pl.semaphore_signal(barrier, 1, device_id=dev(x, y, (z + i) % NZ, c), device_id_type=MESH)
+            pl.semaphore_signal(barrier, 1, device_id=dev(x, y, (z + i) & 15, c), device_id_type=MESH)
 
     pl.semaphore_wait(barrier, 1 + 2 * (NX * NY - 1) + 2 * (NZ - 1))
 
     mine = pair * 2 + core
 
     def x_copy(view, dy, dlo, target):
-        ty = (y + dy) % NY
-        tlo = (xlo + dlo) % 2
+        ty = (y + dy) & 3
+        tlo = (xlo ^ dlo)
         tx = x if dlo == 0 else (x ^ 1 if view == 0 else 3 - x)
         src = (first, second)[view]
         col = pl.multiple_of((ty * 2 + tlo) * PAIR, PAIR)
@@ -103,6 +120,17 @@
         @pl.when(core != view)
         def _():
             x_copy(view, 0, 0, sib).start()
+
+    def x_sent():
+        for dy, dlo in offsets:
+            for view in range(2):
+                x_copy(view, dy, dlo, None).wait_send()
+        for view in range(2):
+            @pl.when(core != view)
+            def _():
+                x_copy(view, 0, 0, sib).wait_send()
+
+    sent.append(x_sent)
 
     w_place = wb.at[pl.ds(pl.multiple_of(core * BLOCK, BLOCK), BLOCK), :]
     w_copy = rcopy(w, w_place, w_s, w_r, sib)
@@ -119,7 +147,7 @@
             own_copy(view).wait()
 
     def chunk_step(dy, dlo):
-        chunk = ((y + dy) % NY) * 2 + (xlo + dlo) % 2
+        chunk = ((y + dy) & 3) * 2 + (xlo ^ dlo)
         for c in range(2):
             b = chunk * 2 + c
             rows = pl.ds(pl.multiple_of(b * 64, 64), 64)
@@ -141,22 +169,24 @@
         ptb[i * OWN:(i + 1) * OWN, :] = (part - jnp.mean(part, 1, keepdims=True)).astype(BF)
 
     def rs_copy(i):
-        ty = (y + i // 2) % NY
-        tlo = (xlo + i % 2) % 2
+        ty = (y + (i >> 1)) & 3
+        tlo = xlo ^ (i & 1)
         rows = pl.ds(pl.multiple_of((ty * 2 + tlo) * OWN, OWN), OWN)
         return rcopy(
             ptb.at[rows, :], rsb.at[pair], rs_s.at[i], rs_r.at[pair], dev(xhi * 2 + tlo, ty, z, core)
         )
 
-    @pl.loop(1, PAIRS)
+    @each(1, PAIRS)
     def _(i):
         rs_copy(i).start()
 
+    when_sent(rs_copy, 1, PAIRS)
+
     rsb[pair] = ptb[pl.ds(pl.multiple_of(pair * OWN, OWN), OWN), :]
 
-    @pl.loop(1, PAIRS)
-    def _(i):
-        other = (pair + i) % PAIRS
+    @each(1, PAIRS)
+    def _(i):
+        other = (pair + i) & 7
         rcopy(rsb.at[other], rsb.at[other], rs_s.at[0], rs_r.at[other], sib).wait_recv()
 
     total = rsb[0].astype(F32)
@@ -177,73 +207,86 @@
     def ag_copy(i):
         return rcopy(
             nt.at[own_rows, :], nt.at[own_rows, :], ag_s.at[i], ag_r.at[place],
-            dev((x + i % NX) % NX, (y + i // NX) % NY, z, core),
+            dev((x + i) & 3, (y + (i >> 2)) & 3, z, core),
         )
 
     def sc_copy(i):
         return rcopy(
             sc.at[pair], sc.at[pair], sc_s.at[i], sc_r.at[pair],
-            dev(xhi * 2 + (xlo + i % 2) % 2, (y + i // 2) % NY, z, core),
-        )
-
-    @pl.loop(1, NX * NY)
+            dev(xhi * 2 + xlo ^ (i & 1), (y + (i >> 1)) & 3, z, core),
+        )
+
+    @each(1, NX * NY)
     def _(i):
         ag_copy(i).start()
 
-    @pl.loop(1, PAIRS)
+    when_sent(ag_copy, 1, NX * NY)
+
+    @each(1, PAIRS)
     def _(i):
         sc_copy(i).start()
 
-    @pl.loop(1, NX * NY)
-    def _(i):
-        sx, sy = (x + i % NX) % NX, (y + i // NX) % NY
-        rows = pl.ds(pl.multiple_of((sx // 2) * SLAB + (sy * 2 + sx % 2) * OWN, OWN), OWN)
+    when_sent(sc_copy, 1, PAIRS)
+
+    @each(1, NX * NY)
+    def _(i):
+        sx, sy = (x + i) & 3, (y + (i >> 2)) & 3
+        rows = pl.ds(pl.multiple_of((sx >> 1) * SLAB + (sy * 2 + (sx & 1)) * OWN, OWN), OWN)
         rcopy(nt.at[rows, :], nt.at[rows, :], ag_s.at[0], ag_r.at[sy * NX + sx], sib).wait_recv()
 
-    kl[...] = nt[:, pl.ds(pl.multiple_of((place // 2) * 128, 128), 128)].T
-    strip = kl[pl.ds(pl.multiple_of((place % 2) * STRIP, STRIP), STRIP), :]
+    @each(1, PAIRS)
+    def _(i):
+        other = (pair + i) & 7
+        rcopy(sc.at[other], sc.at[other], sc_s.at[0], sc_r.at[other], sib).wait_recv()
+
+    kl[...] = nt[:, pl.ds(pl.multiple_of((place >> 1) * 128, 128), 128)].T
+    strip = kl[pl.ds(pl.multiple_of((place & 1) * STRIP, STRIP), STRIP), :]
     for i in range(4):
         kp[:, i * 256:(i + 1) * 256] = jnp.dot(
             strip, nt[:, i * 256:(i + 1) * 256], preferred_element_type=F32
         ).astype(BF)
 
     def piece(ref, t):
-        return ref.at[pl.ds(pl.multiple_of((t // 4) * 16, 16), 16), pl.ds(pl.multiple_of((t % 4) * 256, 256), 256)]
+        return ref.at[pl.ds(pl.multiple_of((t >> 2) * 16, 16), 16), pl.ds(pl.multiple_of((t & 3) * 256, 256), 256)]
 
     def zr_copy(i):
-        t = (z + i) % NZ
+        t = (z + i) & 15
         return rcopy(piece(kp, t), zb.at[z], zr_s.at[i], zr_r.at[z], dev(x, y, t, core))
 
-    @pl.loop(1, NZ)
+    @each(1, NZ)
     def _(i):
         zr_copy(i).start()
+
+    when_sent(zr_copy, 1, NZ)
 
     slab_rows = pl.ds(pl.multiple_of(xhi * SLAB, SLAB), SLAB)
     n_copy = rcopy(nt.at[slab_rows, :], noth, n_s, n_r, sib)
     n_copy.start()
 
     zb[z] = kp[
-        pl.ds(pl.multiple_of((z // 4) * 16, 16), 16), pl.ds(pl.multiple_of((z % 4) * 256, 256), 256)
+        pl.ds(pl.multiple_of((z >> 2) * 16, 16), 16), pl.ds(pl.multiple_of((z & 3) * 256, 256), 256)
     ]
 
-    @pl.loop(1, NZ)
-    def _(i):
-        t = (z + i) % NZ
+    @each(1, NZ)
+    def _(i):
+        t = (z + i) & 15
         rcopy(zb.at[t], zb.at[t], zr_s.at[0], zr_r.at[t], sib).wait_recv()
 
+    n_copy.wait()
     acc = zb[0].astype(F32)
     for i in range(1, NZ):
         acc = acc + zb[i].astype(F32)
     ks[...] = acc.astype(BF)
 
     def za_copy(i):
-        return rcopy(ks, piece(kf, z), za_s.at[i], za_r.at[z], dev(x, y, (z + i) % NZ, 1 - core))
-
-    @pl.loop(0, NZ)
+        return rcopy(ks, piece(kf, z), za_s.at[i], za_r.at[z], dev(x, y, (z + i) & 15, 1 - core))
+
+    @each(0, NZ)
     def _(i):
         za_copy(i).start()
 
-    n_copy.wait()
+    when_sent(za_copy, 0, NZ)
+
     for i in range(8):
         rows = slice(i * 128, (i + 1) * 128)
         nn[rows, :] = nt[slab_rows, rows].T
@@ -255,11 +298,6 @@
     diag = diag / ROWS
     d = -2.0 * (1.0 - diag) - 2.0 * off_weight * diag
 
-    @pl.loop(1, PAIRS)
-    def _(i):
-        other = (pair + i) % PAIRS
-        rcopy(sc.at[other], sc.at[other], sc_s.at[0], sc_r.at[other], sib).wait_recv()
-
     cols = []
     for i in range(PAIRS):
         t = sc[i]
@@ -267,9 +305,9 @@
             cols.append(jnp.broadcast_to(t[:, 32 * j:32 * j + 1], (8, 128)))
     scale_row = jnp.concatenate(cols, 0).T[0:1, :]
 
-    @pl.loop(0, NZ)
-    def _(i):
-        t = (z + i) % NZ
+    @each(0, NZ)
+    def _(i):
+        t = (z + i) & 15
         rcopy(ks, piece(kf, t), za_s.at[0], za_r.at[t], sib).wait_recv()
 
     for h in range(2):
@@ -278,21 +316,23 @@
         ).astype(BF)
 
     def g_copy(i):
-        tx = (x + i % NX) % NX
+        tx = (x + i) & 3
         return rcopy(
-            gs.at[tx // 2], gb.at[pl.ds(pl.multiple_of(place * STRIP, STRIP), STRIP), :], g_s.at[i], g_r.at[place],
-            dev(tx, (y + i // NX) % NY, z, core),
-        )
-
-    @pl.loop(1, NX * NY)
+            gs.at[tx >> 1], gb.at[pl.ds(pl.multiple_of(place * STRIP, STRIP), STRIP), :], g_s.at[i], g_r.at[place],
+            dev(tx, (y + (i >> 2)) & 3, z, core),
+        )
+
+    @each(1, NX * NY)
     def _(i):
         g_copy(i).start()
 
+    when_sent(g_copy, 1, NX * NY)
+
     gb[pl.ds(pl.multiple_of(place * STRIP, STRIP), STRIP), :] = gs[xhi]
 
-    @pl.loop(1, NX * NY)
-    def _(i):
-        t = ((y + i // NX) % NY) * NX + (x + i % NX) % NX
+    @each(1, NX * NY)
+    def _(i):
+        t = ((y + (i >> 2)) & 3) * NX + ((x + i) & 3)
         rows = pl.ds(pl.multiple_of(t * STRIP, STRIP), STRIP)
         rcopy(gb.at[rows, :], gb.at[rows, :], g_s.at[0], g_r.at[t], sib).wait_recv()
 
@@ -325,31 +365,8 @@
     f_copy.wait()
     out[...] += fr[...]
 
-    for dy, dlo in offsets:
-        for view in range(2):
-            x_copy(view, dy, dlo, None).wait_send()
-    for view in range(2):
-        @pl.when(core != view)
-        def _():
-            x_copy(view, 0, 0, sib).wait_send()
-
-    @pl.loop(1, PAIRS)
-    def _(i):
-        rs_copy(i).wait_send()
-        sc_copy(i).wait_send()
-
-    @pl.loop(1, NX * NY)
-    def _(i):
-        ag_copy(i).wait_send()
-        g_copy(i).wait_send()
-
-    @pl.loop(1, NZ)
-    def _(i):
-        zr_copy(i).wait_send()
-
-    @pl.loop(0, NZ)
-    def _(i):
-        za_copy(i).wait_send()
+    for wait in sent:
+        wait()
 
 
 def local(first_view, second_view, weight):

time: 109 us -> 110 us (level)
  no operation moved by 1% of the time
where the time goes in v2:
time: 110 us; the launch traced here: 109 us
  Pallas kernels  105 us (95%)
  local copies, waits for them, and re-layouts  4.19 us (4%)
    pallas_call x1, Pallas kernels, local(): pl.pallas_call(kernel, out_shape=jax.ShapeDtypeStruct((BLOCK, SLAB), F32)...  105 us
    unnamed x7, local copies, waits for them, and re-layouts  4.19 us

profile of v2, /device:TPU:1, one launch (start us, length us, event | category | flops | bytes accessed | tf_op | source)
XLA Modules:
  0.0 109.5 jit_solution(1012852026482743547)
XLA Ops:
  0.0 0.0 copy-start
  0.0 1.2 %copy-done = bf16[64,8192]{1,0:T(8,128)(2,1)S(1)} copy-done((bf16[64,8192]{1,0:T(8,128)(2,1)S(1)}, bf16[64,8192]{1,0:T(8,128)(2,1)}, u32[]{:S(2)}) %copy-start) | copy-done | bytes 1048600
  1.2 0.0 copy-start.1
  1.2 1.2 %copy-done.1 = bf16[64,8192]{1,0:T(8,128)(2,1)S(1)} copy-done((bf16[64,8192]{1,0:T(8,128)(2,1)S(1)}, bf16[64,8192]{1,0:T(8,128)(2,1)}, u32[]{:S(2)}) %copy-start.1) | copy-done | bytes 1048600
  2.5 0.0 copy-start.2
  2.5 0.9 copy-done.2
  3.4 105.3 %shard_map.37 = f32[512,256]{1,0:T(8,128)S(1)} custom-call(bf16[64,8192]{1,0:T(8,128)(2,1)S(1)} %copy-done, bf16[64,8192]{1,0:T(8,128)(2,1)S(1)} %copy-done.1, bf16[512,256]{1,0:T(8,128)(2,1)S(1)} %copy-done.2), custom_call_target="tpu_custom_call" | custom-call | flops 4000000000 | bytes 4194304 | tf_op jit(solution)/shard_map/pallas_call | solution.py:375
  108.7 0.8 copy.5
Async XLA Ops:
  0.0 1.2 %copy-start = (bf16[64,8192]{1,0:T(8,128)(2,1)S(1)}, bf16[64,8192]{1,0:T(8,128)(2,1)}, u32[]{:S(2)}) copy-start(bf16[64,8192]{1,0:T(8,128)(2,1)} %first.1) | copy-start | bytes 3145732
  1.2 1.2 %copy-start.1 = (bf16[64,8192]{1,0:T(8,128)(2,1)S(1)}, bf16[64,8192]{1,0:T(8,128)(2,1)}, u32[]{:S(2)}) copy-start(bf16[64,8192]{1,0:T(8,128)(2,1)} %second.1) | copy-start | bytes 3145732
  2.5 0.9 copy-start.2

commit v3 on v2

--- a/solution.py
+++ b/solution.py
@@ -33,12 +33,22 @@
     return (y * 4 + (x & 1) * 2 + core, z * 2 + (x >> 1))
 
 
-def each(low, high):
+def each(values):
     def run(body):
-        for i in range(low, high):
+        for i in values:
             body(i)
 
     return run
+
+
+def ring(step, size):
+    return min(step, size - step)
+
+
+PLANE_FAR = sorted(range(1, 16), key=lambda i: -ring(i & 3, 4) - ring(i >> 2, 4))
+GROUP_FAR = sorted(range(1, PAIRS), key=lambda i: -(i & 1) - ring(i >> 1, 4))
+X_ORDER = [(2, 1), (1, 1), (3, 1), (2, 0), (1, 0), (3, 0), (0, 1)]
+LINE_FAR = sorted(range(NZ), key=lambda i: -ring(i, NZ))
 
 
 def rcopy(src, dst, send, recv, device):
@@ -50,7 +60,7 @@
 def kernel(
     first, second, w, out,
     xb, xt, wb, wt, pt, ptb, rsb, nt, sc, scb, noth, kl, kp, zb, ks, kf, gs, gb, nn, no, gw, cb, fs, fr,
-    loc, x_s, x_r, w_s, w_r, rs_s, rs_r, ag_s, ag_r, sc_s, sc_r, n_s, n_r, zr_s, zr_r, za_s, za_r, g_s, g_r, f_s, f_r,
+    loc, x_s, x_r, q_s, q_r, w_s, w_r, rs_s, rs_r, ag_s, ag_r, sc_s, sc_r, n_s, n_r, zr_s, zr_r, za_s, za_r, g_s, g_r, f_s, f_r,
 ):
     x, y, z, core = coords()
     xlo, xhi = x & 1, x >> 1
@@ -59,10 +69,9 @@
     sib = dev(x, y, z, 1 - core)
     sent = []
 
-    def when_sent(copy, low, high):
+    def when_sent(copy, values):
         def wait():
-            @each(low, high)
-            def _(i):
+            for i in values:
                 copy(i).wait_send()
 
         sent.append(wait)
@@ -70,14 +79,14 @@
     barrier = pltpu.get_barrier_semaphore()
     pl.semaphore_signal(barrier, 1, device_id=sib, device_id_type=MESH)
 
-    @each(1, NX * NY)
+    @each(PLANE_FAR)
     def _(i):
         for c in range(2):
             pl.semaphore_signal(
                 barrier, 1, device_id=dev((x + i) & 3, (y + (i >> 2)) & 3, z, c), device_id_type=MESH
             )
 
-    @each(1, NZ)
+    @each(LINE_FAR[:-1])
     def _(i):
         for c in range(2):
             pl.semaphore_signal(barrier, 1, device_id=dev(x, y, (z + i) & 15, c), device_id_type=MESH)
@@ -86,32 +95,49 @@
 
     mine = pair * 2 + core
 
-    def x_copy(view, dy, dlo, target):
+    half = z & 1
+
+    def half_cols(h):
+        return pl.ds(pl.multiple_of(h * BLOCK, BLOCK), BLOCK)
+
+    def batch_rows(b):
+        return pl.ds(pl.multiple_of(b * 64, 64), 64)
+
+    def x_copy(view, dy, dlo):
         ty = (y + dy) & 3
-        tlo = (xlo ^ dlo)
+        tlo = xlo ^ dlo
         tx = x if dlo == 0 else (x ^ 1 if view == 0 else 3 - x)
         src = (first, second)[view]
-        col = pl.multiple_of((ty * 2 + tlo) * PAIR, PAIR)
-        return rcopy(
-            src.at[:, pl.ds(col, PAIR)],
-            xb.at[pl.ds(pl.multiple_of(mine * 64, 64), 64), :],
+        col = pl.multiple_of((ty * 2 + tlo) * PAIR + half * BLOCK, BLOCK)
+        return rcopy(
+            src.at[:, pl.ds(col, BLOCK)],
+            xb.at[batch_rows(mine), half_cols(half)],
             x_s.at[(dy * 2 + dlo) * 2 + view],
             x_r.at[mine],
-            dev(tx, ty, z, view) if target is None else target,
+            dev(tx, ty, z, view),
+        )
+
+    def sib_copy(view):
+        src = (first, second)[view]
+        return rcopy(
+            src.at[:, pl.ds(pl.multiple_of(pair * PAIR, PAIR), PAIR)],
+            xb.at[batch_rows(mine), :],
+            x_s.at[0],
+            x_r.at[mine],
+            sib,
         )
 
     def own_copy(view):
         src = (first, second)[view]
         return pltpu.make_async_copy(
             src.at[:, pl.ds(pl.multiple_of(pair * PAIR, PAIR), PAIR)],
-            xb.at[pl.ds(pl.multiple_of(mine * 64, 64), 64), :],
+            xb.at[batch_rows(mine), :],
             loc.at[0],
         )
 
-    offsets = [(dy, dlo) for dy in (2, 1, 3, 0) for dlo in (1, 0) if (dy, dlo) != (0, 0)]
-    for dy, dlo in offsets:
+    for dy, dlo in X_ORDER:
         for view in range(2):
-            x_copy(view, dy, dlo, None).start()
+            x_copy(view, dy, dlo).start()
     for view in range(2):
         @pl.when(core == view)
         def _():
@@ -119,16 +145,16 @@
 
         @pl.when(core != view)
         def _():
-            x_copy(view, 0, 0, sib).start()
+            sib_copy(view).start()
 
     def x_sent():
-        for dy, dlo in offsets:
+        for dy, dlo in X_ORDER:
             for view in range(2):
-                x_copy(view, dy, dlo, None).wait_send()
+                x_copy(view, dy, dlo).wait_send()
         for view in range(2):
             @pl.when(core != view)
             def _():
-                x_copy(view, 0, 0, sib).wait_send()
+                sib_copy(view).wait_send()
 
     sent.append(x_sent)
 
@@ -141,28 +167,54 @@
     w_copy.wait()
     for i in range(PAIR // SLAB):
         wt[:, i * SLAB:(i + 1) * SLAB] = wb[i * SLAB:(i + 1) * SLAB, :].T
+    def chunk_of(dy, dlo):
+        return ((y + dy) & 3) * 2 + (xlo ^ dlo)
+
+    def relay(dy, dlo, c):
+        b = chunk_of(dy, dlo) * 2 + c
+        place_there = xb.at[batch_rows(b), half_cols(half)]
+        return rcopy(
+            place_there, place_there, q_s.at[(dy * 2 + dlo) * 2 + c], q_r.at[b],
+            dev(x, y, (z + (1 if c == 0 else 15)) & 15, core),
+        )
+
+    def product_of(chunk, h, add):
+        rows = pl.ds(pl.multiple_of(chunk * 128, 128), 128)
+        xs = xb[rows, half_cols(h)]
+        part = lax.dot_general(wt[:, half_cols(h)], xs, ROW_DIMS, preferred_element_type=F32)
+        pt[:, rows] = pt[:, rows] + part if add else part
+        xt[half_cols(h), rows] = xs.T
+
+    for dy, dlo in X_ORDER:
+        for c in range(2):
+            b = chunk_of(dy, dlo) * 2 + c
+            got = xb.at[batch_rows(b), half_cols(half)]
+            rcopy(got, got, x_s.at[0], x_r.at[b], sib).wait_recv()
+            relay(dy, dlo, c).start()
+        product_of(chunk_of(dy, dlo), half, False)
+
+    def relay_sent():
+        for dy, dlo in X_ORDER:
+            for c in range(2):
+                relay(dy, dlo, c).wait_send()
+
+    sent.append(relay_sent)
+
     for view in range(2):
         @pl.when(core == view)
         def _():
             own_copy(view).wait()
-
-    def chunk_step(dy, dlo):
-        chunk = ((y + dy) & 3) * 2 + (xlo ^ dlo)
+    got = xb.at[batch_rows(pair * 2 + 1 - core), :]
+    rcopy(got, got, x_s.at[0], x_r.at[pair * 2 + 1 - core], sib).wait_recv()
+    product_of(pair, half, False)
+    product_of(pair, 1 - half, True)
+
+    for dy, dlo in X_ORDER:
         for c in range(2):
-            b = chunk * 2 + c
-            rows = pl.ds(pl.multiple_of(b * 64, 64), 64)
-
-            @pl.when(b != mine)
-            def _():
-                rcopy(xb.at[rows, :], xb.at[rows, :], x_s.at[0], x_r.at[b], sib).wait_recv()
-
-        rows = pl.ds(pl.multiple_of(chunk * 128, 128), 128)
-        xs = xb[rows, :]
-        pt[:, rows] = lax.dot_general(wt[...], xs, ROW_DIMS, preferred_element_type=F32)
-        xt[:, rows] = xs.T
-
-    for dy, dlo in [(0, 0), (0, 1), (1, 0), (3, 0), (1, 1), (3, 1), (2, 0), (2, 1)]:
-        chunk_step(dy, dlo)
+            b = chunk_of(dy, dlo) * 2 + c
+            got = xb.at[batch_rows(b), half_cols(1 - half)]
+            rcopy(got, got, q_s.at[0], q_r.at[b], sib).wait_recv()
+        product_of(chunk_of(dy, dlo), 1 - half, True)
 
     for i in range(PAIRS):
         part = pt[i * OWN:(i + 1) * OWN, :]
@@ -176,15 +228,15 @@
             ptb.at[rows, :], rsb.at[pair], rs_s.at[i], rs_r.at[pair], dev(xhi * 2 + tlo, ty, z, core)
         )
 
-    @each(1, PAIRS)
+    @each(GROUP_FAR)
     def _(i):
         rs_copy(i).start()
 
-    when_sent(rs_copy, 1, PAIRS)
+    when_sent(rs_copy, GROUP_FAR)
 
     rsb[pair] = ptb[pl.ds(pl.multiple_of(pair * OWN, OWN), OWN), :]
 
-    @each(1, PAIRS)
+    @each(GROUP_FAR)
     def _(i):
         other = (pair + i) & 7
         rcopy(rsb.at[other], rsb.at[other], rs_s.at[0], rs_r.at[other], sib).wait_recv()
@@ -216,25 +268,25 @@
             dev(xhi * 2 + xlo ^ (i & 1), (y + (i >> 1)) & 3, z, core),
         )
 
-    @each(1, NX * NY)
+    @each(PLANE_FAR)
     def _(i):
         ag_copy(i).start()
 
-    when_sent(ag_copy, 1, NX * NY)
-
-    @each(1, PAIRS)
+    when_sent(ag_copy, PLANE_FAR)
+
+    @each(GROUP_FAR)
     def _(i):
         sc_copy(i).start()
 
-    when_sent(sc_copy, 1, PAIRS)
-
-    @each(1, NX * NY)
+    when_sent(sc_copy, GROUP_FAR)
+
+    @each(PLANE_FAR)
     def _(i):
         sx, sy = (x + i) & 3, (y + (i >> 2)) & 3
         rows = pl.ds(pl.multiple_of((sx >> 1) * SLAB + (sy * 2 + (sx & 1)) * OWN, OWN), OWN)
         rcopy(nt.at[rows, :], nt.at[rows, :], ag_s.at[0], ag_r.at[sy * NX + sx], sib).wait_recv()
 
-    @each(1, PAIRS)
+    @each(GROUP_FAR)
     def _(i):
         other = (pair + i) & 7
         rcopy(sc.at[other], sc.at[other], sc_s.at[0], sc_r.at[other], sib).wait_recv()
@@ -253,11 +305,11 @@
         t = (z + i) & 15
         return rcopy(piece(kp, t), zb.at[z], zr_s.at[i], zr_r.at[z], dev(x, y, t, core))
 
-    @each(1, NZ)
+    @each(LINE_FAR[:-1])
     def _(i):
         zr_copy(i).start()
 
-    when_sent(zr_copy, 1, NZ)
+    when_sent(zr_copy, LINE_FAR[:-1])
 
     slab_rows = pl.ds(pl.multiple_of(xhi * SLAB, SLAB), SLAB)
     n_copy = rcopy(nt.at[slab_rows, :], noth, n_s, n_r, sib)
@@ -267,7 +319,7 @@
         pl.ds(pl.multiple_of((z >> 2) * 16, 16), 16), pl.ds(pl.multiple_of((z & 3) * 256, 256), 256)
     ]
 
-    @each(1, NZ)
+    @each(LINE_FAR[:-1])
     def _(i):
         t = (z + i) & 15
         rcopy(zb.at[t], zb.at[t], zr_s.at[0], zr_r.at[t], sib).wait_recv()
@@ -281,11 +333,11 @@
     def za_copy(i):
         return rcopy(ks, piece(kf, z), za_s.at[i], za_r.at[z], dev(x, y, (z + i) & 15, 1 - core))
 
-    @each(0, NZ)
+    @each(LINE_FAR)
     def _(i):
         za_copy(i).start()
 
-    when_sent(za_copy, 0, NZ)
+    when_sent(za_copy, LINE_FAR)
 
     for i in range(8):
         rows = slice(i * 128, (i + 1) * 128)
@@ -305,7 +357,7 @@
             cols.append(jnp.broadcast_to(t[:, 32 * j:32 * j + 1], (8, 128)))
     scale_row = jnp.concatenate(cols, 0).T[0:1, :]
 
-    @each(0, NZ)
+    @each(LINE_FAR)
     def _(i):
         t = (z + i) & 15
         rcopy(ks, piece(kf, t), za_s.at[0], za_r.at[t], sib).wait_recv()
@@ -322,15 +374,15 @@
             dev(tx, (y + (i >> 2)) & 3, z, core),
         )
 
-    @each(1, NX * NY)
+    @each(PLANE_FAR)
     def _(i):
         g_copy(i).start()
 
-    when_sent(g_copy, 1, NX * NY)
+    when_sent(g_copy, PLANE_FAR)
 
     gb[pl.ds(pl.multiple_of(place * STRIP, STRIP), STRIP), :] = gs[xhi]
 
-    @each(1, NX * NY)
+    @each(PLANE_FAR)
     def _(i):
         t = ((y + (i >> 2)) & 3) * NX + ((x + i) & 3)
         rows = pl.ds(pl.multiple_of(t * STRIP, STRIP), STRIP)
@@ -384,11 +436,11 @@
             vm((STRIP, ROWS), BF), vm((NZ, 16, 256), BF), vm((16, 256), BF), vm((STRIP, ROWS), BF),
             vm((2, STRIP, SLAB), BF), vm((ROWS, SLAB), BF), vm((ROWS, SLAB), BF), vm((ROWS, SLAB), BF),
             vm((ROWS, SLAB), F32), vm((ROWS, SLAB), BF), vm((BLOCK, SLAB), F32), vm((BLOCK, SLAB), F32),
-            dma((2,)), dma((16,)), dma((16,)), dma, dma, dma((PAIRS,)), dma((PAIRS,)), dma((16,)), dma((16,)),
+            dma((2,)), dma((16,)), dma((16,)), dma((16,)), dma((16,)), dma, dma, dma((PAIRS,)), dma((PAIRS,)), dma((16,)), dma((16,)),
             dma((PAIRS,)), dma((PAIRS,)), dma, dma, dma((NZ,)), dma((NZ,)), dma((NZ,)), dma((NZ,)),
             dma((16,)), dma((16,)), dma, dma,
         ],
-        compiler_params=pltpu.CompilerParams(collective_id=0, has_side_effects=True, vmem_limit_bytes=48 << 20),
+        compiler_params=pltpu.CompilerParams(collective_id=0, has_side_effects=True, vmem_limit_bytes=62 << 20),
         cost_estimate=pl.CostEstimate(flops=4 * 10**9, bytes_accessed=4 << 20, transcendentals=0),
     )(first_view, second_view, weight)
 

time: 110 us -> 90.5 us (0.82)
  Pallas kernels: 105 us -> 88.5 us
  local copies, waits for them, and re-layouts: 4.19 us -> 1.87 us
    pallas_call x1, Pallas kernels: 105 us -> 88.5 us  [local(): pl.pallas_call(kernel, out_shape=jax.ShapeDtypeStruct((BLOCK, SLAB), F32)...]
    unnamed x7 -> x1, local copies, waits for them, and re-layouts: 4.19 us -> 1.87 us
where the time goes in v3:
time: 90.5 us; the launch traced here: 90.3 us
  Pallas kernels  88.5 us (98%)
  local copies, waits for them, and re-layouts  1.87 us (2%)
    pallas_call x1, Pallas kernels, local(): pl.pallas_call(kernel, out_shape=jax.ShapeDtypeStruct((BLOCK, SLAB), F32)...  88.5 us
    unnamed x1, local copies, waits for them, and re-layouts  1.87 us

profile of v3, /device:TPU:1, one launch (start us, length us, event | category | flops | bytes accessed | tf_op | source)
XLA Modules:
  0.0 90.3 jit_solution(14733285771739779727)
XLA Ops:
  0.0 88.5 %shard_map.37 = f32[512,256]{1,0:T(8,128)} custom-call(bf16[64,8192]{1,0:T(8,128)(2,1)} %first.1, bf16[64,8192]{1,0:T(8,128)(2,1)} %second.1, bf16[512,256]{1,0:T(8,128)(2,1)} %w.1), custom_call_target="tpu_custom_call" | custom-call | flops 4000000000 | bytes 4194304 | tf_op jit(solution)/shard_map/pallas_call | solution.py:427
  88.5 1.9 %copy.5 = f32[512,256]{1,0:T(8,128)} copy(f32[512,256]{1,0:T(8,128)} %shard_map.37) | data formatting | bytes 1048576

commit v4 on v3

--- a/solution.py
+++ b/solution.py
@@ -16,6 +16,7 @@
 PAIR = 2 * BLOCK
 PAIRS = 8
 OWN = SLAB // PAIRS
+HALF_OWN = OWN // 2
 STRIP = ROWS // (NX * NY)
 BF = jnp.bfloat16
 F32 = jnp.float32
@@ -47,7 +48,8 @@
 
 PLANE_FAR = sorted(range(1, 16), key=lambda i: -ring(i & 3, 4) - ring(i >> 2, 4))
 GROUP_FAR = sorted(range(1, PAIRS), key=lambda i: -(i & 1) - ring(i >> 1, 4))
-X_ORDER = [(2, 1), (1, 1), (3, 1), (2, 0), (1, 0), (3, 0), (0, 1)]
+X_ORDER = [(1, 1), (3, 1), (1, 0), (3, 0), (2, 1), (2, 0), (0, 1)]
+WHOLE = [(0, 1)]
 LINE_FAR = sorted(range(NZ), key=lambda i: -ring(i, NZ))
 
 
@@ -108,10 +110,15 @@
         tlo = xlo ^ dlo
         tx = x if dlo == 0 else (x ^ 1 if view == 0 else 3 - x)
         src = (first, second)[view]
-        col = pl.multiple_of((ty * 2 + tlo) * PAIR + half * BLOCK, BLOCK)
-        return rcopy(
-            src.at[:, pl.ds(col, BLOCK)],
-            xb.at[batch_rows(mine), half_cols(half)],
+        if (dy, dlo) in WHOLE:
+            col = pl.ds(pl.multiple_of((ty * 2 + tlo) * PAIR, PAIR), PAIR)
+            there = xb.at[batch_rows(mine), :]
+        else:
+            col = pl.ds(pl.multiple_of((ty * 2 + tlo) * PAIR + half * BLOCK, BLOCK), BLOCK)
+            there = xb.at[batch_rows(mine), half_cols(half)]
+        return rcopy(
+            src.at[:, col],
+            there,
             x_s.at[(dy * 2 + dlo) * 2 + view],
             x_r.at[mine],
             dev(tx, ty, z, view),
@@ -188,13 +195,21 @@
     for dy, dlo in X_ORDER:
         for c in range(2):
             b = chunk_of(dy, dlo) * 2 + c
-            got = xb.at[batch_rows(b), half_cols(half)]
-            rcopy(got, got, x_s.at[0], x_r.at[b], sib).wait_recv()
-            relay(dy, dlo, c).start()
+            if (dy, dlo) in WHOLE:
+                got = xb.at[batch_rows(b), :]
+                rcopy(got, got, x_s.at[0], x_r.at[b], sib).wait_recv()
+            else:
+                got = xb.at[batch_rows(b), half_cols(half)]
+                rcopy(got, got, x_s.at[0], x_r.at[b], sib).wait_recv()
+                relay(dy, dlo, c).start()
         product_of(chunk_of(dy, dlo), half, False)
+        if (dy, dlo) in WHOLE:
+            product_of(chunk_of(dy, dlo), 1 - half, True)
+
+    relayed = [offset for offset in X_ORDER if offset not in WHOLE]
 
     def relay_sent():
-        for dy, dlo in X_ORDER:
+        for dy, dlo in relayed:
             for c in range(2):
                 relay(dy, dlo, c).wait_send()
 
@@ -209,46 +224,60 @@
     product_of(pair, half, False)
     product_of(pair, 1 - half, True)
 
-    for dy, dlo in X_ORDER:
+    for dy, dlo in relayed:
         for c in range(2):
             b = chunk_of(dy, dlo) * 2 + c
             got = xb.at[batch_rows(b), half_cols(1 - half)]
             rcopy(got, got, q_s.at[0], q_r.at[b], sib).wait_recv()
         product_of(chunk_of(dy, dlo), 1 - half, True)
 
-    for i in range(PAIRS):
-        part = pt[i * OWN:(i + 1) * OWN, :]
-        ptb[i * OWN:(i + 1) * OWN, :] = (part - jnp.mean(part, 1, keepdims=True)).astype(BF)
-
-    def rs_copy(i):
+    def rs_copy(k):
+        i, part = k & 7, k >> 3
         ty = (y + (i >> 1)) & 3
         tlo = xlo ^ (i & 1)
-        rows = pl.ds(pl.multiple_of((ty * 2 + tlo) * OWN, OWN), OWN)
-        return rcopy(
-            ptb.at[rows, :], rsb.at[pair], rs_s.at[i], rs_r.at[pair], dev(xhi * 2 + tlo, ty, z, core)
-        )
-
-    @each(GROUP_FAR)
-    def _(i):
-        rs_copy(i).start()
-
-    when_sent(rs_copy, GROUP_FAR)
-
-    rsb[pair] = ptb[pl.ds(pl.multiple_of(pair * OWN, OWN), OWN), :]
-
-    @each(GROUP_FAR)
-    def _(i):
-        other = (pair + i) & 7
-        rcopy(rsb.at[other], rsb.at[other], rs_s.at[0], rs_r.at[other], sib).wait_recv()
-
-    total = rsb[0].astype(F32)
-    for i in range(1, PAIRS):
-        total = total + rsb[i].astype(F32)
-    mean = jnp.sum(total, 1, keepdims=True) / ROWS
-    spread = jnp.sum(total * total, 1, keepdims=True) / ROWS - mean * mean
-    scale = lax.rsqrt(spread + 1e-05)
-    own_rows = pl.ds(pl.multiple_of(xhi * SLAB + pair * OWN, OWN), OWN)
-    nt[own_rows, :] = ((total - mean) * scale).astype(BF)
+        rows = pl.ds(pl.multiple_of((ty * 2 + tlo) * OWN + part * HALF_OWN, HALF_OWN), HALF_OWN)
+        return rcopy(
+            ptb.at[rows, :], rsb.at[pair, part], rs_s.at[k], rs_r.at[part * PAIRS + pair],
+            dev(xhi * 2 + tlo, ty, z, core),
+        )
+
+    def own_rows(part):
+        return pl.ds(pl.multiple_of(xhi * SLAB + pair * OWN + part * HALF_OWN, HALF_OWN), HALF_OWN)
+
+    def ag_copy(k):
+        i, part = k & 15, k >> 4
+        return rcopy(
+            nt.at[own_rows(part), :], nt.at[own_rows(part), :], ag_s.at[k], ag_r.at[part * 16 + place],
+            dev((x + i) & 3, (y + (i >> 2)) & 3, z, core),
+        )
+
+    for part in range(2):
+        for i in range(PAIRS):
+            rows = slice(i * OWN + part * HALF_OWN, i * OWN + (part + 1) * HALF_OWN)
+            values = pt[rows, :]
+            ptb[rows, :] = (values - jnp.mean(values, 1, keepdims=True)).astype(BF)
+        for i in GROUP_FAR:
+            rs_copy(part * PAIRS + i).start()
+        when_sent(rs_copy, [part * PAIRS + i for i in GROUP_FAR])
+
+    scales = []
+    for part in range(2):
+        rsb[pair, part] = ptb[pl.ds(pl.multiple_of(pair * OWN + part * HALF_OWN, HALF_OWN), HALF_OWN), :]
+        for i in GROUP_FAR:
+            other = (pair + i) & 7
+            got = rsb.at[other, part]
+            rcopy(got, got, rs_s.at[0], rs_r.at[part * PAIRS + other], sib).wait_recv()
+        total = rsb[0, part].astype(F32)
+        for i in range(1, PAIRS):
+            total = total + rsb[i, part].astype(F32)
+        mean = jnp.sum(total, 1, keepdims=True) / ROWS
+        spread = jnp.sum(total * total, 1, keepdims=True) / ROWS - mean * mean
+        scales.append(lax.rsqrt(spread + 1e-05))
+        nt[own_rows(part), :] = ((total - mean) * scales[part]).astype(BF)
+        for i in PLANE_FAR:
+            ag_copy(part * 16 + i).start()
+        when_sent(ag_copy, [part * 16 + i for i in PLANE_FAR])
+    scale = jnp.concatenate(scales, 0)
     lane = lax.broadcasted_iota(jnp.int32, (8, 128), 1)
     wide = jnp.broadcast_to(scale, (OWN, 128))
     tile = wide[0:8]
@@ -256,35 +285,24 @@
         tile = jnp.where(lane >= 32 * i, wide[8 * i:8 * i + 8], tile)
     sc[pair] = tile
 
-    def ag_copy(i):
-        return rcopy(
-            nt.at[own_rows, :], nt.at[own_rows, :], ag_s.at[i], ag_r.at[place],
-            dev((x + i) & 3, (y + (i >> 2)) & 3, z, core),
-        )
-
     def sc_copy(i):
         return rcopy(
             sc.at[pair], sc.at[pair], sc_s.at[i], sc_r.at[pair],
             dev(xhi * 2 + xlo ^ (i & 1), (y + (i >> 1)) & 3, z, core),
         )
 
-    @each(PLANE_FAR)
-    def _(i):
-        ag_copy(i).start()
-
-    when_sent(ag_copy, PLANE_FAR)
-
     @each(GROUP_FAR)
     def _(i):
         sc_copy(i).start()
 
     when_sent(sc_copy, GROUP_FAR)
 
-    @each(PLANE_FAR)
-    def _(i):
-        sx, sy = (x + i) & 3, (y + (i >> 2)) & 3
-        rows = pl.ds(pl.multiple_of((sx >> 1) * SLAB + (sy * 2 + (sx & 1)) * OWN, OWN), OWN)
-        rcopy(nt.at[rows, :], nt.at[rows, :], ag_s.at[0], ag_r.at[sy * NX + sx], sib).wait_recv()
+    for part in range(2):
+        for i in PLANE_FAR:
+            sx, sy = (x + i) & 3, (y + (i >> 2)) & 3
+            first_row = (sx >> 1) * SLAB + (sy * 2 + (sx & 1)) * OWN + part * HALF_OWN
+            got = nt.at[pl.ds(pl.multiple_of(first_row, HALF_OWN), HALF_OWN), :]
+            rcopy(got, got, ag_s.at[0], ag_r.at[part * 16 + sy * NX + sx], sib).wait_recv()
 
     @each(GROUP_FAR)
     def _(i):
@@ -431,12 +449,12 @@
         out_specs=pl.BlockSpec(memory_space=pltpu.VMEM),
         scratch_shapes=[
             vm((ROWS, PAIR), BF), vm((PAIR, ROWS), BF), vm((PAIR, SLAB), BF), vm((SLAB, PAIR), BF),
-            vm((SLAB, ROWS), F32), vm((SLAB, ROWS), BF), vm((PAIRS, OWN, ROWS), BF), vm((2 * SLAB, ROWS), BF),
+            vm((SLAB, ROWS), F32), vm((SLAB, ROWS), BF), vm((PAIRS, 2, HALF_OWN, ROWS), BF), vm((2 * SLAB, ROWS), BF),
             vm((PAIRS, 8, 128), F32), vm((8, 128), F32), vm((SLAB, ROWS), BF), vm((128, 2 * SLAB), BF),
             vm((STRIP, ROWS), BF), vm((NZ, 16, 256), BF), vm((16, 256), BF), vm((STRIP, ROWS), BF),
             vm((2, STRIP, SLAB), BF), vm((ROWS, SLAB), BF), vm((ROWS, SLAB), BF), vm((ROWS, SLAB), BF),
             vm((ROWS, SLAB), F32), vm((ROWS, SLAB), BF), vm((BLOCK, SLAB), F32), vm((BLOCK, SLAB), F32),
-            dma((2,)), dma((16,)), dma((16,)), dma((16,)), dma((16,)), dma, dma, dma((PAIRS,)), dma((PAIRS,)), dma((16,)), dma((16,)),
+            dma((2,)), dma((16,)), dma((16,)), dma((16,)), dma((16,)), dma, dma, dma((16,)), dma((16,)), dma((32,)), dma((32,)),
             dma((PAIRS,)), dma((PAIRS,)), dma, dma, dma((NZ,)), dma((NZ,)), dma((NZ,)), dma((NZ,)),
             dma((16,)), dma((16,)), dma, dma,
         ],

time: 90.5 us -> 89.5 us (0.989)
  Pallas kernels: 88.5 us -> 87.5 us
    pallas_call x1, Pallas kernels: 88.5 us -> 87.5 us  [local(): pl.pallas_call(kernel, out_shape=jax.ShapeDtypeStruct((BLOCK, SLAB), F32)...]
where the time goes in v4:
time: 89.5 us; the launch traced here: 89.3 us
  Pallas kernels  87.5 us (98%)
  local copies, waits for them, and re-layouts  1.87 us (2%)
    pallas_call x1, Pallas kernels, local(): pl.pallas_call(kernel, out_shape=jax.ShapeDtypeStruct((BLOCK, SLAB), F32)...  87.5 us
    unnamed x1, local copies, waits for them, and re-layouts  1.87 us

profile of v4, /device:TPU:1, one launch (start us, length us, event | category | flops | bytes accessed | tf_op | source)
XLA Modules:
  0.0 89.3 jit_solution(11924314081304493765)
XLA Ops:
  0.0 87.5 %shard_map.37 = f32[512,256]{1,0:T(8,128)} custom-call(bf16[64,8192]{1,0:T(8,128)(2,1)} %first.1, bf16[64,8192]{1,0:T(8,128)(2,1)} %second.1, bf16[512,256]{1,0:T(8,128)(2,1)} %w.1), custom_call_target="tpu_custom_call" | custom-call | flops 4000000000 | bytes 4194304 | tf_op jit(solution)/shard_map/pallas_call | solution.py:445
  87.5 1.9 %copy.5 = f32[512,256]{1,0:T(8,128)} copy(f32[512,256]{1,0:T(8,128)} %shard_map.37) | data formatting | bytes 1048576

commit v5 on v4

--- a/solution.py
+++ b/solution.py
@@ -17,6 +17,7 @@
 PAIRS = 8
 OWN = SLAB // PAIRS
 HALF_OWN = OWN // 2
+HALF_SLAB = SLAB // 2
 STRIP = ROWS // (NX * NY)
 BF = jnp.bfloat16
 F32 = jnp.float32
@@ -63,6 +64,7 @@
     first, second, w, out,
     xb, xt, wb, wt, pt, ptb, rsb, nt, sc, scb, noth, kl, kp, zb, ks, kf, gs, gb, nn, no, gw, cb, fs, fr,
     loc, x_s, x_r, q_s, q_r, w_s, w_r, rs_s, rs_r, ag_s, ag_r, sc_s, sc_r, n_s, n_r, zr_s, zr_r, za_s, za_r, g_s, g_r, f_s, f_r,
+    sw_s, sw_r, ns_s, ns_r, ns, ka,
 ):
     x, y, z, core = coords()
     xlo, xhi = x & 1, x >> 1
@@ -91,7 +93,7 @@
     @each(LINE_FAR[:-1])
     def _(i):
         for c in range(2):
-            pl.semaphore_signal(barrier, 1, device_id=dev(x, y, (z + i) & 15, c), device_id_type=MESH)
+            pl.semaphore_signal(barrier, 1, device_id=dev(x ^ c, y, (z + i) & 15, core), device_id_type=MESH)
 
     pl.semaphore_wait(barrier, 1 + 2 * (NX * NY - 1) + 2 * (NZ - 1))
 
@@ -231,29 +233,52 @@
             rcopy(got, got, q_s.at[0], q_r.at[b], sib).wait_recv()
         product_of(chunk_of(dy, dlo), 1 - half, True)
 
+    def part_rows(part, p):
+        return pl.ds(pl.multiple_of(part * HALF_SLAB + p * HALF_OWN, HALF_OWN), HALF_OWN)
+
     def rs_copy(k):
         i, part = k & 7, k >> 3
         ty = (y + (i >> 1)) & 3
         tlo = xlo ^ (i & 1)
-        rows = pl.ds(pl.multiple_of((ty * 2 + tlo) * OWN + part * HALF_OWN, HALF_OWN), HALF_OWN)
-        return rcopy(
-            ptb.at[rows, :], rsb.at[pair, part], rs_s.at[k], rs_r.at[part * PAIRS + pair],
+        return rcopy(
+            ptb.at[part_rows(part, ty * 2 + tlo), :], rsb.at[pair, part], rs_s.at[k], rs_r.at[part * PAIRS + pair],
             dev(xhi * 2 + tlo, ty, z, core),
         )
 
-    def own_rows(part):
-        return pl.ds(pl.multiple_of(xhi * SLAB + pair * OWN + part * HALF_OWN, HALF_OWN), HALF_OWN)
+    def plane_rows(h, part, p):
+        return pl.ds(pl.multiple_of(h * SLAB + part * HALF_SLAB + p * HALF_OWN, HALF_OWN), HALF_OWN)
 
     def ag_copy(k):
-        i, part = k & 15, k >> 4
-        return rcopy(
-            nt.at[own_rows(part), :], nt.at[own_rows(part), :], ag_s.at[k], ag_r.at[part * 16 + place],
-            dev((x + i) & 3, (y + (i >> 2)) & 3, z, core),
-        )
+        part, h, dy = k >> 3, (k >> 2) & 1, k & 3
+        return rcopy(
+            ns.at[part_rows(part, pair), :], nt.at[plane_rows(xhi, part, pair), :], ag_s.at[k],
+            ag_r.at[part * PAIRS + pair], dev(core + 2 * h, (y + dy) & 3, z, xhi),
+        )
+
+    alone = jnp.logical_and(core == xlo, core == xhi)
+
+    def ag_far(part):
+        return [part * 8 + h * 4 + dy for dy in (2, 1, 3, 0) for h in range(2)]
+
+    def unless_mine(k, do):
+        if k & 3 == 0:
+            h = (k >> 2) & 1
+
+            @pl.when(jnp.logical_not(jnp.logical_and(alone, xhi == h)))
+            def _():
+                do(ag_copy(k))
+        else:
+            do(ag_copy(k))
+
+    def ag_sent():
+        for k in range(16):
+            unless_mine(k, lambda copy: copy.wait_send())
+
+    sent.append(ag_sent)
 
     for part in range(2):
         for i in range(PAIRS):
-            rows = slice(i * OWN + part * HALF_OWN, i * OWN + (part + 1) * HALF_OWN)
+            rows = slice(part * HALF_SLAB + i * HALF_OWN, part * HALF_SLAB + (i + 1) * HALF_OWN)
             values = pt[rows, :]
             ptb[rows, :] = (values - jnp.mean(values, 1, keepdims=True)).astype(BF)
         for i in GROUP_FAR:
@@ -262,7 +287,7 @@
 
     scales = []
     for part in range(2):
-        rsb[pair, part] = ptb[pl.ds(pl.multiple_of(pair * OWN + part * HALF_OWN, HALF_OWN), HALF_OWN), :]
+        rsb[pair, part] = ptb[part_rows(part, pair), :]
         for i in GROUP_FAR:
             other = (pair + i) & 7
             got = rsb.at[other, part]
@@ -273,10 +298,15 @@
         mean = jnp.sum(total, 1, keepdims=True) / ROWS
         spread = jnp.sum(total * total, 1, keepdims=True) / ROWS - mean * mean
         scales.append(lax.rsqrt(spread + 1e-05))
-        nt[own_rows(part), :] = ((total - mean) * scales[part]).astype(BF)
-        for i in PLANE_FAR:
-            ag_copy(part * 16 + i).start()
-        when_sent(ag_copy, [part * 16 + i for i in PLANE_FAR])
+        normed = ((total - mean) * scales[part]).astype(BF)
+        ns[part_rows(part, pair), :] = normed
+
+        @pl.when(alone)
+        def _():
+            nt[plane_rows(xhi, part, pair), :] = normed
+
+        for k in ag_far(part):
+            unless_mine(k, lambda copy: copy.start())
     scale = jnp.concatenate(scales, 0)
     lane = lax.broadcasted_iota(jnp.int32, (8, 128), 1)
     wide = jnp.broadcast_to(scale, (OWN, 128))
@@ -297,24 +327,45 @@
 
     when_sent(sc_copy, GROUP_FAR)
 
+    strip_place = (y * 2 + xhi) * 2 + core
+    lanes = pl.ds(pl.multiple_of((strip_place >> 1) * 128, 128), 128)
+
+    def swap(part):
+        rows = pl.ds(pl.multiple_of(core * SLAB + part * HALF_SLAB, HALF_SLAB), HALF_SLAB)
+        return rcopy(nt.at[rows, :], nt.at[rows, :], sw_s.at[part], sw_r.at[part], sib)
+
     for part in range(2):
-        for i in PLANE_FAR:
-            sx, sy = (x + i) & 3, (y + (i >> 2)) & 3
-            first_row = (sx >> 1) * SLAB + (sy * 2 + (sx & 1)) * OWN + part * HALF_OWN
-            got = nt.at[pl.ds(pl.multiple_of(first_row, HALF_OWN), HALF_OWN), :]
-            rcopy(got, got, ag_s.at[0], ag_r.at[part * 16 + sy * NX + sx], sib).wait_recv()
+        for i in GROUP_FAR + [0]:
+            other = (pair + i) & 7
+            got = nt.at[plane_rows(core, part, other), :]
+
+            def arrived():
+                rcopy(got, got, ag_s.at[0], ag_r.at[part * PAIRS + other], sib).wait_recv()
+
+            if i == 0:
+                pl.when(jnp.logical_not(alone))(arrived)
+            else:
+                arrived()
+        swap(part).start()
+        swap(part).wait()
+        for h in range(2):
+            columns = slice(h * SLAB + part * HALF_SLAB, h * SLAB + (part + 1) * HALF_SLAB)
+            kl[h] = nt[columns, lanes].T
+            strip = kl[h, pl.ds(pl.multiple_of(core * STRIP, STRIP), STRIP), :]
+            for i in range(4):
+                cols = slice(i * 256, (i + 1) * 256)
+                term = jnp.dot(strip, nt[columns, cols], preferred_element_type=F32)
+                if part == 0 and h == 0:
+                    ka[:, cols] = term
+                elif part == 1 and h == 1:
+                    kp[:, cols] = (ka[:, cols] + term).astype(BF)
+                else:
+                    ka[:, cols] += term
 
     @each(GROUP_FAR)
     def _(i):
         other = (pair + i) & 7
         rcopy(sc.at[other], sc.at[other], sc_s.at[0], sc_r.at[other], sib).wait_recv()
-
-    kl[...] = nt[:, pl.ds(pl.multiple_of((place >> 1) * 128, 128), 128)].T
-    strip = kl[pl.ds(pl.multiple_of((place & 1) * STRIP, STRIP), STRIP), :]
-    for i in range(4):
-        kp[:, i * 256:(i + 1) * 256] = jnp.dot(
-            strip, nt[:, i * 256:(i + 1) * 256], preferred_element_type=F32
-        ).astype(BF)
 
     def piece(ref, t):
         return ref.at[pl.ds(pl.multiple_of((t >> 2) * 16, 16), 16), pl.ds(pl.multiple_of((t & 3) * 256, 256), 256)]
@@ -329,9 +380,18 @@
 
     when_sent(zr_copy, LINE_FAR[:-1])
 
-    slab_rows = pl.ds(pl.multiple_of(xhi * SLAB, SLAB), SLAB)
-    n_copy = rcopy(nt.at[slab_rows, :], noth, n_s, n_r, sib)
-    n_copy.start()
+    def ns_copy(k):
+        i, part = k & 7, k >> 3
+        rows = part_rows(part, pair)
+        return rcopy(
+            ns.at[rows, :], ns.at[rows, :], ns_s.at[k], ns_r.at[part * PAIRS + pair],
+            dev(xhi * 2 + (xlo ^ (i & 1)), (y + (i >> 1)) & 3, z, core),
+        )
+
+    ns_all = [part * PAIRS + i for i in GROUP_FAR for part in range(2)]
+    for k in ns_all:
+        ns_copy(k).start()
+    when_sent(ns_copy, ns_all)
 
     zb[z] = kp[
         pl.ds(pl.multiple_of((z >> 2) * 16, 16), 16), pl.ds(pl.multiple_of((z & 3) * 256, 256), 256)
@@ -342,14 +402,13 @@
         t = (z + i) & 15
         rcopy(zb.at[t], zb.at[t], zr_s.at[0], zr_r.at[t], sib).wait_recv()
 
-    n_copy.wait()
     acc = zb[0].astype(F32)
     for i in range(1, NZ):
         acc = acc + zb[i].astype(F32)
     ks[...] = acc.astype(BF)
 
     def za_copy(i):
-        return rcopy(ks, piece(kf, z), za_s.at[i], za_r.at[z], dev(x, y, (z + i) & 15, 1 - core))
+        return rcopy(ks, piece(kf, z), za_s.at[i], za_r.at[z], dev(x ^ 1, y, (z + i) & 15, core))
 
     @each(LINE_FAR)
     def _(i):
@@ -357,9 +416,19 @@
 
     when_sent(za_copy, LINE_FAR)
 
+    for k in ns_all:
+        i, part = k & 7, k >> 3
+        other = (pair + i) & 7
+        got = ns.at[part_rows(part, other), :]
+        rcopy(got, got, ns_s.at[0], ns_r.at[part * PAIRS + other], sib).wait_recv()
+    n_copy = rcopy(ns, noth, n_s, n_r, sib)
+    n_copy.start()
     for i in range(8):
         rows = slice(i * 128, (i + 1) * 128)
-        nn[rows, :] = nt[slab_rows, rows].T
+        nn[rows, :] = ns[:, rows].T
+    n_copy.wait()
+    for i in range(8):
+        rows = slice(i * 128, (i + 1) * 128)
         no[rows, :] = noth[:, rows].T
     diag = jnp.zeros((1, SLAB), F32)
     for i in range(8):
@@ -369,42 +438,58 @@
     d = -2.0 * (1.0 - diag) - 2.0 * off_weight * diag
 
     cols = []
-    for i in range(PAIRS):
-        t = sc[i]
-        for j in range(OWN // 8):
-            cols.append(jnp.broadcast_to(t[:, 32 * j:32 * j + 1], (8, 128)))
+    for part in range(2):
+        for i in range(PAIRS):
+            t = sc[i]
+            for j in (2 * part, 2 * part + 1):
+                cols.append(jnp.broadcast_to(t[:, 32 * j:32 * j + 1], (8, 128)))
     scale_row = jnp.concatenate(cols, 0).T[0:1, :]
 
-    @each(LINE_FAR)
-    def _(i):
+    for i in LINE_FAR:
         t = (z + i) & 15
         rcopy(ks, piece(kf, t), za_s.at[0], za_r.at[t], sib).wait_recv()
+
+    def g_rows(s):
+        return pl.ds(pl.multiple_of(s * STRIP, STRIP), STRIP)
+
+    def g_copy(i):
+        tx = (x + i) & 3
+        return rcopy(
+            gs.at[tx >> 1], gb.at[g_rows(strip_place), :], g_s.at[i], g_r.at[strip_place],
+            dev(tx, (y + (i >> 2)) & 3, z, xlo),
+        )
 
     for h in range(2):
         gs[h] = lax.dot_general(
             kf[...], nt[h * SLAB:(h + 1) * SLAB, :], ROW_DIMS, preferred_element_type=F32
         ).astype(BF)
-
-    def g_copy(i):
-        tx = (x + i) & 3
-        return rcopy(
-            gs.at[tx >> 1], gb.at[pl.ds(pl.multiple_of(place * STRIP, STRIP), STRIP), :], g_s.at[i], g_r.at[place],
-            dev(tx, (y + (i >> 2)) & 3, z, core),
-        )
-
-    @each(PLANE_FAR)
-    def _(i):
+    for i in PLANE_FAR:
         g_copy(i).start()
 
-    when_sent(g_copy, PLANE_FAR)
-
-    gb[pl.ds(pl.multiple_of(place * STRIP, STRIP), STRIP), :] = gs[xhi]
-
-    @each(PLANE_FAR)
-    def _(i):
-        t = ((y + (i >> 2)) & 3) * NX + ((x + i) & 3)
-        rows = pl.ds(pl.multiple_of(t * STRIP, STRIP), STRIP)
-        rcopy(gb.at[rows, :], gb.at[rows, :], g_s.at[0], g_r.at[t], sib).wait_recv()
+    @pl.when(core == xlo)
+    def _():
+        gb[g_rows(strip_place), :] = gs[xhi]
+
+    @pl.when(core != xlo)
+    def _():
+        g_copy(0).start()
+
+    def g_sent():
+        for i in PLANE_FAR:
+            g_copy(i).wait_send()
+
+        @pl.when(core != xlo)
+        def _():
+            g_copy(0).wait_send()
+
+    sent.append(g_sent)
+
+    for s in range(16):
+        def arrived():
+            got = gb.at[g_rows(s), :]
+            rcopy(got, got, g_s.at[0], g_r.at[s], sib).wait_recv()
+
+        pl.when(jnp.logical_or(core != xlo, strip_place != s))(arrived)
 
     g_sum = jnp.zeros((1, SLAB), F32)
     gn_sum = jnp.zeros((1, SLAB), F32)
@@ -426,14 +511,19 @@
         rows = pl.ds(pl.multiple_of(block * BLOCK + i * 128, 128), 128)
         return jnp.dot(xt[rows, :], cb[...], preferred_element_type=F32) * factor
 
+    def f_copy(i):
+        rows = pl.ds(i * 128, 128)
+        return rcopy(fs.at[rows, :], fr.at[rows, :], f_s.at[i], f_r.at[i], sib)
+
     for i in range(4):
         fs[i * 128:(i + 1) * 128, :] = product(1 - core, i)
-    f_copy = rcopy(fs, fr, f_s, f_r, sib)
-    f_copy.start()
+        f_copy(i).start()
+    when_sent(f_copy, range(4))
     for i in range(4):
-        out[i * 128:(i + 1) * 128, :] = product(core, i)
-    f_copy.wait()
-    out[...] += fr[...]
+        rows = slice(i * 128, (i + 1) * 128)
+        part = product(core, i)
+        f_copy(i).wait_recv()
+        out[rows, :] = part + fr[rows, :]
 
     for wait in sent:
         wait()
@@ -450,15 +540,16 @@
         scratch_shapes=[
             vm((ROWS, PAIR), BF), vm((PAIR, ROWS), BF), vm((PAIR, SLAB), BF), vm((SLAB, PAIR), BF),
             vm((SLAB, ROWS), F32), vm((SLAB, ROWS), BF), vm((PAIRS, 2, HALF_OWN, ROWS), BF), vm((2 * SLAB, ROWS), BF),
-            vm((PAIRS, 8, 128), F32), vm((8, 128), F32), vm((SLAB, ROWS), BF), vm((128, 2 * SLAB), BF),
+            vm((PAIRS, 8, 128), F32), vm((8, 128), F32), vm((SLAB, ROWS), BF), vm((2, 128, HALF_SLAB), BF),
             vm((STRIP, ROWS), BF), vm((NZ, 16, 256), BF), vm((16, 256), BF), vm((STRIP, ROWS), BF),
             vm((2, STRIP, SLAB), BF), vm((ROWS, SLAB), BF), vm((ROWS, SLAB), BF), vm((ROWS, SLAB), BF),
             vm((ROWS, SLAB), F32), vm((ROWS, SLAB), BF), vm((BLOCK, SLAB), F32), vm((BLOCK, SLAB), F32),
-            dma((2,)), dma((16,)), dma((16,)), dma((16,)), dma((16,)), dma, dma, dma((16,)), dma((16,)), dma((32,)), dma((32,)),
+            dma((2,)), dma((16,)), dma((16,)), dma((16,)), dma((16,)), dma, dma, dma((16,)), dma((16,)), dma((16,)), dma((16,)),
             dma((PAIRS,)), dma((PAIRS,)), dma, dma, dma((NZ,)), dma((NZ,)), dma((NZ,)), dma((NZ,)),
-            dma((16,)), dma((16,)), dma, dma,
+            dma((16,)), dma((16,)), dma((4,)), dma((4,)),
+            dma((2,)), dma((2,)), dma((16,)), dma((16,)), vm((SLAB, ROWS), BF), vm((STRIP, ROWS), F32),
         ],
-        compiler_params=pltpu.CompilerParams(collective_id=0, has_side_effects=True, vmem_limit_bytes=62 << 20),
+        compiler_params=pltpu.CompilerParams(collective_id=0, has_side_effects=True, vmem_limit_bytes=53 << 20),
         cost_estimate=pl.CostEstimate(flops=4 * 10**9, bytes_accessed=4 << 20, transcendentals=0),
     )(first_view, second_view, weight)
 

time: 89.5 us -> 85 us (0.950)
  Pallas kernels: 87.5 us -> 83.1 us
    pallas_call x1, Pallas kernels: 87.5 us -> 83.1 us  [local(): pl.pallas_call(kernel, out_shape=jax.ShapeDtypeStruct((BLOCK, SLAB), F32)...]
    unnamed x1 -> x3, local copies, waits for them, and re-layouts: 1.87 us -> 1.75 us
where the time goes in v5:
time: 85 us; the launch traced here: 84.9 us
  Pallas kernels  83.1 us (98%)
  local copies, waits for them, and re-layouts  1.75 us (2%)
    pallas_call x1, Pallas kernels, local(): pl.pallas_call(kernel, out_shape=jax.ShapeDtypeStruct((BLOCK, SLAB), F32)...  83.1 us
    unnamed x3, local copies, waits for them, and re-layouts  1.75 us

profile of v5, /device:TPU:1, one launch (start us, length us, event | category | flops | bytes accessed | tf_op | source)
XLA Modules:
  0.0 84.9 jit_solution(9666460478140277387)
XLA Ops:
  0.0 0.0 copy-start
  0.0 0.9 %copy-done = bf16[512,256]{1,0:T(8,128)(2,1)S(1)} copy-done((bf16[512,256]{1,0:T(8,128)(2,1)S(1)}, bf16[512,256]{1,0:T(8,128)(2,1)}, u32[]{:S(2)}) %copy-start) | copy-done | bytes 262168
  1.0 83.1 %shard_map.37 = f32[512,256]{1,0:T(8,128)S(1)} custom-call(bf16[64,8192]{1,0:T(8,128)(2,1)} %first.1, bf16[64,8192]{1,0:T(8,128)(2,1)} %second.1, bf16[512,256]{1,0:T(8,128)(2,1)S(1)} %copy-done), custom_call_target="tpu_custom_call" | custom-call | flops 4000000000 | bytes 4194304 | tf_op jit(solution)/shard_map/pallas_call | solution.py:535
  84.1 0.8 copy.5
Async XLA Ops:
  0.0 0.9 %copy-start = (bf16[512,256]{1,0:T(8,128)(2,1)S(1)}, bf16[512,256]{1,0:T(8,128)(2,1)}, u32[]{:S(2)}) copy-start(bf16[512,256]{1,0:T(8,128)(2,1)} %w.1) | copy-start | bytes 786436

commit v6 on v5

--- a/solution.py
+++ b/solution.py
@@ -64,7 +64,7 @@
     first, second, w, out,
     xb, xt, wb, wt, pt, ptb, rsb, nt, sc, scb, noth, kl, kp, zb, ks, kf, gs, gb, nn, no, gw, cb, fs, fr,
     loc, x_s, x_r, q_s, q_r, w_s, w_r, rs_s, rs_r, ag_s, ag_r, sc_s, sc_r, n_s, n_r, zr_s, zr_r, za_s, za_r, g_s, g_r, f_s, f_r,
-    sw_s, sw_r, ns_s, ns_r, ns, ka,
+    sw_s, sw_r, ns_s, ns_r, ns, ka, line_sem,
 ):
     x, y, z, core = coords()
     xlo, xhi = x & 1, x >> 1
@@ -90,12 +90,20 @@
                 barrier, 1, device_id=dev((x + i) & 3, (y + (i >> 2)) & 3, z, c), device_id_type=MESH
             )
 
-    @each(LINE_FAR[:-1])
-    def _(i):
+    for i in (1, NZ - 1):
         for c in range(2):
             pl.semaphore_signal(barrier, 1, device_id=dev(x ^ c, y, (z + i) & 15, core), device_id_type=MESH)
 
-    pl.semaphore_wait(barrier, 1 + 2 * (NX * NY - 1) + 2 * (NZ - 1))
+    pl.semaphore_wait(barrier, 1 + 2 * (NX * NY - 1) + 4)
+
+    def tell(i):
+        for step in (1 << i, NZ - (1 << i)):
+            pl.semaphore_signal(line_sem.at[i], 1, device_id=dev(x, y, (z + step) & 15, core), device_id_type=MESH)
+
+    def hear(i):
+        pl.semaphore_wait(line_sem.at[i], 2)
+
+    tell(0)
 
     mine = pair * 2 + core
 
@@ -226,6 +234,8 @@
     product_of(pair, half, False)
     product_of(pair, 1 - half, True)
 
+    hear(0)
+    tell(1)
     for dy, dlo in relayed:
         for c in range(2):
             b = chunk_of(dy, dlo) * 2 + c
@@ -285,6 +295,8 @@
             rs_copy(part * PAIRS + i).start()
         when_sent(rs_copy, [part * PAIRS + i for i in GROUP_FAR])
 
+    hear(1)
+    tell(2)
     scales = []
     for part in range(2):
         rsb[pair, part] = ptb[part_rows(part, pair), :]
@@ -366,6 +378,8 @@
     def _(i):
         other = (pair + i) & 7
         rcopy(sc.at[other], sc.at[other], sc_s.at[0], sc_r.at[other], sib).wait_recv()
+
+    hear(2)
 
     def piece(ref, t):
         return ref.at[pl.ds(pl.multiple_of((t >> 2) * 16, 16), 16), pl.ds(pl.multiple_of((t & 3) * 256, 256), 256)]
@@ -548,6 +562,7 @@
             dma((PAIRS,)), dma((PAIRS,)), dma, dma, dma((NZ,)), dma((NZ,)), dma((NZ,)), dma((NZ,)),
             dma((16,)), dma((16,)), dma((4,)), dma((4,)),
             dma((2,)), dma((2,)), dma((16,)), dma((16,)), vm((SLAB, ROWS), BF), vm((STRIP, ROWS), F32),
+            pltpu.SemaphoreType.REGULAR((3,)),
         ],
         compiler_params=pltpu.CompilerParams(collective_id=0, has_side_effects=True, vmem_limit_bytes=53 << 20),
         cost_estimate=pl.CostEstimate(flops=4 * 10**9, bytes_accessed=4 << 20, transcendentals=0),

time: 85 us -> 82.3 us (0.968)
  Pallas kernels: 83.1 us -> 80.4 us
    pallas_call x1, Pallas kernels: 83.1 us -> 80.4 us  [local(): pl.pallas_call(kernel, out_shape=jax.ShapeDtypeStruct((BLOCK, SLAB), F32)...]
where the time goes in v6:
time: 82.3 us; the launch traced here: 82.1 us
  Pallas kernels  80.4 us (98%)
  local copies, waits for them, and re-layouts  1.75 us (2%)
    pallas_call x1, Pallas kernels, local(): pl.pallas_call(kernel, out_shape=jax.ShapeDtypeStruct((BLOCK, SLAB), F32)...  80.4 us
    unnamed x3, local copies, waits for them, and re-layouts  1.75 us

profile of v6, /device:TPU:1, one launch (start us, length us, event | category | flops | bytes accessed | tf_op | source)
XLA Modules:
  0.0 82.1 jit_solution(608751695630910815)
XLA Ops:
  0.0 0.0 copy-start
  0.0 0.9 %copy-done = bf16[512,256]{1,0:T(8,128)(2,1)S(1)} copy-done((bf16[512,256]{1,0:T(8,128)(2,1)S(1)}, bf16[512,256]{1,0:T(8,128)(2,1)}, u32[]{:S(2)}) %copy-start) | copy-done | bytes 262168
  1.0 80.4 %shard_map.37 = f32[512,256]{1,0:T(8,128)S(1)} custom-call(bf16[64,8192]{1,0:T(8,128)(2,1)} %first.1, bf16[64,8192]{1,0:T(8,128)(2,1)} %second.1, bf16[512,256]{1,0:T(8,128)(2,1)S(1)} %copy-done), custom_call_target="tpu_custom_call" | custom-call | flops 4000000000 | bytes 4194304 | tf_op jit(solution)/shard_map/pallas_call | solution.py:549
  81.3 0.8 copy.5
Async XLA Ops:
  0.0 0.9 %copy-start = (bf16[512,256]{1,0:T(8,128)(2,1)S(1)}, bf16[512,256]{1,0:T(8,128)(2,1)}, u32[]{:S(2)}) copy-start(bf16[512,256]{1,0:T(8,128)(2,1)} %w.1) | copy-start | bytes 786436

commit v7 on v6

--- a/solution.py
+++ b/solution.py
@@ -200,7 +200,8 @@
         xs = xb[rows, half_cols(h)]
         part = lax.dot_general(wt[:, half_cols(h)], xs, ROW_DIMS, preferred_element_type=F32)
         pt[:, rows] = pt[:, rows] + part if add else part
-        xt[half_cols(h), rows] = xs.T
+        if not add:
+            xt[half_cols(h), rows] = xs.T
 
     for dy, dlo in X_ORDER:
         for c in range(2):
@@ -406,6 +407,10 @@
     for k in ns_all:
         ns_copy(k).start()
     when_sent(ns_copy, ns_all)
+
+    for i in range(ROWS // 128):
+        rows = slice(i * 128, (i + 1) * 128)
+        xt[half_cols(1 - half), rows] = xb[rows, half_cols(1 - half)].T
 
     zb[z] = kp[
         pl.ds(pl.multiple_of((z >> 2) * 16, 16), 16), pl.ds(pl.multiple_of((z & 3) * 256, 256), 256)

time: 82.3 us -> 82.6 us (level)
  no operation moved by 1% of the time
where the time goes in v7:
time: 82.6 us; the launch traced here: 82.4 us
  Pallas kernels  80.7 us (98%)
  local copies, waits for them, and re-layouts  1.75 us (2%)
    pallas_call x1, Pallas kernels, local(): pl.pallas_call(kernel, out_shape=jax.ShapeDtypeStruct((BLOCK, SLAB), F32)...  80.7 us
    unnamed x3, local copies, waits for them, and re-layouts  1.75 us

profile of v7, /device:TPU:1, one launch (start us, length us, event | category | flops | bytes accessed | tf_op | source)
XLA Modules:
  0.0 82.4 jit_solution(1223683304312375658)
XLA Ops:
  0.0 0.0 copy-start
  0.0 0.9 %copy-done = bf16[512,256]{1,0:T(8,128)(2,1)S(1)} copy-done((bf16[512,256]{1,0:T(8,128)(2,1)S(1)}, bf16[512,256]{1,0:T(8,128)(2,1)}, u32[]{:S(2)}) %copy-start) | copy-done | bytes 262168
  1.0 80.7 %shard_map.37 = f32[512,256]{1,0:T(8,128)S(1)} custom-call(bf16[64,8192]{1,0:T(8,128)(2,1)} %first.1, bf16[64,8192]{1,0:T(8,128)(2,1)} %second.1, bf16[512,256]{1,0:T(8,128)(2,1)S(1)} %copy-done), custom_call_target="tpu_custom_call" | custom-call | flops 4000000000 | bytes 4194304 | tf_op jit(solution)/shard_map/pallas_call | solution.py:554
  81.7 0.8 copy.5
Async XLA Ops:
  0.0 0.9 %copy-start = (bf16[512,256]{1,0:T(8,128)(2,1)S(1)}, bf16[512,256]{1,0:T(8,128)(2,1)}, u32[]{:S(2)}) copy-start(bf16[512,256]{1,0:T(8,128)(2,1)} %w.1) | copy-start | bytes 786436
